TPU v7x, 32 devices: a whole 2x2x4 slice. The times are simulated.
32 devices in a mesh: fsdp: 32 (over z, y, x, core).
Axes of the slice: x: 2, y: 2, z: 4, core: 2. Of those that a mesh axis runs over, the one named last changes fastest.
Arguments:
- hidden: bfloat16 [8192, 768], P('fsdp'), may hold values from -6 to 6
- cotangent: bfloat16 [8192, 768], P('fsdp'), may hold values from -6 to 6
- seq_lengths: int32 [64], P('fsdp'), may hold values from 0 to 256, as said below
- w_qkv: bfloat16 [768, 2304], P('fsdp'), may hold values from -0.21875 to 0.21875
- b_qv: bfloat16 [1536], P('fsdp'), may hold values from -4 to 4
- w_out: bfloat16 [768, 768], P('fsdp'), may hold values from -1.25 to 1.25
- b_out: bfloat16 [768], P('fsdp'), may hold values from -3 to 3
- gain_one: bfloat16 [768], P('fsdp'), may hold values from 0.25 to 1.75
- shift_one: bfloat16 [768], P('fsdp'), may hold values from -3 to 3
- w_in: bfloat16 [768, 3072], P('fsdp'), may hold values from -0.21875 to 0.21875
- b_in: bfloat16 [3072], P('fsdp'), may hold values from -3 to 3
- w_back: bfloat16 [3072, 768], P('fsdp'), may hold values from -0.109375 to 0.109375
- b_back: bfloat16 [768], P('fsdp'), may hold values from -3 to 3
- gain_two: bfloat16 [768], P('fsdp'), may hold values from 0.25 to 1.75
- shift_two: bfloat16 [768], P('fsdp'), may hold values from -3 to 3
Outputs:
- output: bfloat16 [8192, 768], P('fsdp')
- grad_hidden: bfloat16 [8192, 768], P('fsdp')
- grad_w_qkv: float32 [768, 2304], P('fsdp')
- grad_b_qv: float32 [1536], P('fsdp')
- grad_w_out: float32 [768, 768], P('fsdp')
- grad_b_out: float32 [768], P('fsdp')
- grad_gain_one: float32 [768], P('fsdp')
- grad_shift_one: float32 [768], P('fsdp')
- grad_w_in: float32 [768, 3072], P('fsdp')
- grad_b_in: float32 [3072], P('fsdp')
- grad_w_back: float32 [3072, 768], P('fsdp')
- grad_b_back: float32 [768], P('fsdp')
- grad_gain_two: float32 [768], P('fsdp')
- grad_shift_two: float32 [768], P('fsdp')
Inputs may be any that keep to these rules, and one draw needn't show every extreme that they name: `seq_lengths`: block 0 of every device's 2 blocks begins a sequence; a sequence of length L that begins at block j lies within the device's blocks, and the next nonzero entry comes at block j + ceil(L / 128) or later. Some device holds one sequence of 256 tokens.
All inputs are finite; a program needn't handle non-finite values.
Results may differ from a plain program's by a relative error of at most 0.014.
Values may be sent and summed in bfloat16 or wider, within the bound.
A program may use at most 128 MiB of HBM per device.

v0:
```python
import jax
import jax.numpy as jnp
from jax import lax
from jax.sharding import PartitionSpec as P

HEAD_DIM = 64


EPSILON = 1e-12


def layer_norm(values, gain, shift):
    centre = values - jnp.mean(values, axis=-1, keepdims=True)
    spread = jnp.mean(centre * centre, axis=-1, keepdims=True)
    return centre * lax.rsqrt(spread + EPSILON) * gain + shift


def smooth_gate(values):
    return jax.nn.gelu(values, approximate=False)


def seq_masks(lengths, row_count):
    blocks = lengths.shape[0]
    block_width = row_count // blocks
    block_ids = jnp.arange(blocks, dtype=jnp.int32)
    starts = jnp.where(lengths > 0, block_ids, 0)
    owners = lax.cummax(starts, axis=0)
    position = jnp.arange(row_count, dtype=jnp.int32)
    member = position[:, None] // block_width == block_ids[None, :]
    owner_row = jnp.sum(jnp.where(member, owners[None, :], 0), axis=1)
    chosen = owner_row[:, None] == block_ids[None, :]
    length_row = jnp.sum(jnp.where(chosen, lengths[None, :], 0), axis=1)
    alive_row = position - owner_row * block_width < length_row
    same_seq = (owner_row[:, None] == owner_row[None, :]) & alive_row[None, :]
    return (alive_row, same_seq)


def outer_sum(left, right):
    return lax.dot_general(
        left, right, (((0,), (0,)), ((), ())), preferred_element_type=jnp.float32
    )


def column_term(left, right):
    return outer_sum(left, right)


def back_product(grad, weight):
    return lax.dot_general(
        grad, weight, (((1,), (1,)), ((), ())), preferred_element_type=jnp.float32
    )


def masked_scores(queries, keys_all, same_seq, factor):
    raw = jnp.einsum("qhd,khd->hqk", queries, keys_all, preferred_element_type=jnp.float32) * factor
    return jnp.where(same_seq[None], raw, -1e30)


def shards(
    hidden,
    cotangent,
    seq_lengths,
    w_qkv,
    b_qv,
    w_out,
    b_out,
    gain_one,
    shift_one,
    w_in,
    b_in,
    w_back,
    b_back,
    gain_two,
    shift_two,
):
    row_count, model_width = hidden.shape
    head_count = model_width // HEAD_DIM
    factor = HEAD_DIM ** (-0.5)
    alive_row, same_seq = seq_masks(seq_lengths, row_count)
    alive_col = alive_row.astype(jnp.float32)[:, None]
    gathered = (
        lax.all_gather(w_qkv, "fsdp", axis=0, tiled=True),
        lax.all_gather(b_qv, "fsdp", axis=0, tiled=True),
        lax.all_gather(w_out, "fsdp", axis=0, tiled=True),
        lax.all_gather(b_out, "fsdp", axis=0, tiled=True),
        lax.all_gather(gain_one, "fsdp", axis=0, tiled=True),
        lax.all_gather(shift_one, "fsdp", axis=0, tiled=True),
        lax.all_gather(w_in, "fsdp", axis=0, tiled=True),
        lax.all_gather(b_in, "fsdp", axis=0, tiled=True),
        lax.all_gather(w_back, "fsdp", axis=0, tiled=True),
        lax.all_gather(b_back, "fsdp", axis=0, tiled=True),
        lax.all_gather(gain_two, "fsdp", axis=0, tiled=True),
        lax.all_gather(shift_two, "fsdp", axis=0, tiled=True),
    )
    (
        full_qkv,
        full_bqv,
        full_out,
        full_bout,
        full_gone,
        full_sone,
        full_in,
        full_bin,
        full_back,
        full_bback,
        full_gtwo,
        full_stwo,
    ) = gathered
    bias_qv = full_bqv.astype(jnp.float32)
    bias_qkv = jnp.concatenate(
        [bias_qv[:model_width], jnp.zeros((model_width,), jnp.float32), bias_qv[model_width:]]
    )
    qkv_low = (jnp.dot(hidden, full_qkv, preferred_element_type=jnp.float32) + bias_qkv).astype(
        jnp.bfloat16
    )
    queries = qkv_low[:, :model_width].reshape(row_count, head_count, HEAD_DIM)
    keys_all = qkv_low[:, model_width : 2 * model_width].reshape(row_count, head_count, HEAD_DIM)
    values_all = qkv_low[:, 2 * model_width :].reshape(row_count, head_count, HEAD_DIM)
    scores = masked_scores(queries, keys_all, same_seq, factor)
    highest = jnp.max(scores, axis=-1, keepdims=True)
    expo = jnp.exp(scores - highest)
    totals = jnp.sum(expo, axis=-1, keepdims=True)
    log_total = highest + jnp.log(totals)
    probs_low = (expo / totals).astype(jnp.bfloat16)
    attended = jnp.einsum(
        "hqk,khd->qhd", probs_low, values_all, preferred_element_type=jnp.float32
    ).reshape(row_count, model_width)
    attended_low = (attended * alive_col).astype(jnp.bfloat16)
    summed_one = (
        hidden.astype(jnp.float32)
        + jnp.dot(attended_low, full_out, preferred_element_type=jnp.float32)
        + full_bout.astype(jnp.float32)
    )
    normed_one = layer_norm(
        summed_one, full_gone.astype(jnp.float32), full_sone.astype(jnp.float32)
    )
    normed_low = normed_one.astype(jnp.bfloat16)
    inner = jnp.dot(normed_low, full_in, preferred_element_type=jnp.float32) + full_bin.astype(
        jnp.float32
    )
    gated_low = smooth_gate(inner).astype(jnp.bfloat16)
    summed_two = (
        normed_one
        + jnp.dot(gated_low, full_back, preferred_element_type=jnp.float32)
        + full_bback.astype(jnp.float32)
    )
    output = (
        layer_norm(summed_two, full_gtwo.astype(jnp.float32), full_stwo.astype(jnp.float32))
        * alive_col
    ).astype(jnp.bfloat16)
    again = (
        lax.all_gather(w_qkv, "fsdp", axis=0, tiled=True),
        lax.all_gather(w_out, "fsdp", axis=0, tiled=True),
        lax.all_gather(w_in, "fsdp", axis=0, tiled=True),
        lax.all_gather(w_back, "fsdp", axis=0, tiled=True),
        lax.all_gather(gain_one, "fsdp", axis=0, tiled=True),
        lax.all_gather(gain_two, "fsdp", axis=0, tiled=True),
    )
    back_qkv, back_out, back_in, back_back, back_gone, back_gtwo = again
    shift_zero = jnp.zeros((model_width,), jnp.float32)
    unused, norm_two_back = jax.vjp(
        layer_norm, summed_two, back_gtwo.astype(jnp.float32), shift_zero
    )
    grad_sum_two, grad_gtwo, grad_stwo = norm_two_back(cotangent.astype(jnp.float32) * alive_col)
    grad_branch_two = grad_sum_two.astype(jnp.bfloat16)
    share_back = lax.psum_scatter(
        column_term(gated_low, grad_branch_two), "fsdp", scatter_dimension=0, tiled=True
    )
    term_bback = jnp.sum(grad_branch_two.astype(jnp.float32), axis=0)
    grad_gated = back_product(grad_branch_two, back_back)
    unused, gate_back = jax.vjp(smooth_gate, inner)
    grad_inner = gate_back(grad_gated)[0].astype(jnp.bfloat16)
    term_bin = jnp.sum(grad_inner.astype(jnp.float32), axis=0)
    grad_normed = grad_sum_two + back_product(grad_inner, back_in)
    unused, norm_one_back = jax.vjp(
        layer_norm, summed_one, back_gone.astype(jnp.float32), shift_zero
    )
    grad_sum_one, grad_gone, grad_sone = norm_one_back(grad_normed)
    grad_branch_one = grad_sum_one.astype(jnp.bfloat16)
    term_bout = jnp.sum(grad_branch_one.astype(jnp.float32), axis=0)
    grad_attended = (
        (back_product(grad_branch_one, back_out) * alive_col)
        .astype(jnp.bfloat16)
        .reshape(row_count, head_count, HEAD_DIM)
    )
    scores_again = masked_scores(queries, keys_all, same_seq, factor)
    probs = jnp.exp(scores_again - log_total)
    probs_again_low = probs.astype(jnp.bfloat16)
    grad_probs = jnp.einsum(
        "qhd,khd->hqk", grad_attended, values_all, preferred_element_type=jnp.float32
    )
    inner_dot = jnp.sum(probs * grad_probs, axis=-1, keepdims=True)
    grad_scores = jnp.where(same_seq[None], probs * (grad_probs - inner_dot), 0.0).astype(
        jnp.bfloat16
    )
    grad_queries = (
        jnp.einsum("hqk,khd->qhd", grad_scores, keys_all, preferred_element_type=jnp.float32)
        * factor
    )
    grad_keys = (
        jnp.einsum("hqk,qhd->khd", grad_scores, queries, preferred_element_type=jnp.float32)
        * factor
    )
    grad_values = jnp.einsum(
        "hqk,qhd->khd", probs_again_low, grad_attended, preferred_element_type=jnp.float32
    )
    grad_qkv = jnp.concatenate(
        [
            grad_queries.reshape(row_count, model_width),
            grad_keys.reshape(row_count, model_width),
            grad_values.reshape(row_count, model_width),
        ],
        axis=1,
    ).astype(jnp.bfloat16)
    column_sums = jnp.sum(grad_qkv.astype(jnp.float32), axis=0)
    term_bqv = jnp.concatenate([column_sums[:model_width], column_sums[2 * model_width :]])
    grad_hidden = (grad_sum_one + back_product(grad_qkv, back_qkv)).astype(jnp.bfloat16)
    share_all = lax.psum_scatter(
        jnp.concatenate(
            [
                column_term(hidden, grad_qkv),
                column_term(attended_low, grad_branch_one),
                column_term(normed_low, grad_inner),
            ],
            axis=1,
        ),
        "fsdp",
        scatter_dimension=0,
        tiled=True,
    )
    share_qkv = share_all[:, : 3 * model_width]
    share_out = share_all[:, 3 * model_width : 4 * model_width]
    share_in = share_all[:, 4 * model_width :]
    vectors = (
        lax.psum_scatter(term_bqv, "fsdp", scatter_dimension=0, tiled=True),
        lax.psum_scatter(term_bout, "fsdp", scatter_dimension=0, tiled=True),
        lax.psum_scatter(grad_gone, "fsdp", scatter_dimension=0, tiled=True),
        lax.psum_scatter(grad_sone, "fsdp", scatter_dimension=0, tiled=True),
        lax.psum_scatter(term_bin, "fsdp", scatter_dimension=0, tiled=True),
        lax.psum_scatter(term_bback, "fsdp", scatter_dimension=0, tiled=True),
        lax.psum_scatter(grad_gtwo, "fsdp", scatter_dimension=0, tiled=True),
        lax.psum_scatter(grad_stwo, "fsdp", scatter_dimension=0, tiled=True),
    )
    return (
        output,
        grad_hidden,
        share_qkv,
        vectors[0],
        share_out,
        vectors[1],
        vectors[2],
        vectors[3],
        share_in,
        vectors[4],
        share_back,
        vectors[5],
        vectors[6],
        vectors[7],
    )


def solution(mesh):
    return jax.shard_map(
        shards,
        mesh=mesh,
        in_specs=(
            P("fsdp", None),
            P("fsdp", None),
            P("fsdp"),
            P("fsdp", None),
            P("fsdp"),
            P("fsdp", None),
            P("fsdp"),
            P("fsdp"),
            P("fsdp"),
            P("fsdp", None),
            P("fsdp"),
            P("fsdp", None),
            P("fsdp"),
            P("fsdp"),
            P("fsdp"),
        ),
        out_specs=(
            P("fsdp", None),
            P("fsdp", None),
            P("fsdp", None),
            P("fsdp"),
            P("fsdp", None),
            P("fsdp"),
            P("fsdp"),
            P("fsdp"),
            P("fsdp", None),
            P("fsdp"),
            P("fsdp", None),
            P("fsdp"),
            P("fsdp"),
            P("fsdp"),
        ),
        check_vma=False,
    )
```

profile of v0, /device:TPU:3, one launch (start us, length us, event | category | flops | bytes accessed | tf_op | source)
XLA Modules:
  0.0 677.4 jit_solution(12990709529213203961)
XLA Ops:
  16.8 40.0 %all-reduce.17 = (bf16[3072]{0:T(1024)(128)(2,1)S(1)}, bf16[768]{0:T(1024)(128)(2,1)S(1)}, bf16[1536]{0:T(1024)(128)(2,1)S(1)}, bf16[768]{0:T(1024)(128)(2,1)S(1...) all-reduce(bf16[3072]{0:T(1024)(128)(2,1)S(1)} %dynamic-update-slic, ...), channel_id=1, replica_groups=mesh['fsdp'=32] {'fsdp'}, use_global_device_ids=true, to_apply=%add.4 | all-reduce | flops 9216 | bytes 36864
  61.7 11.1 %all-gather.5.cloned.1.call-done = bf16[768,2304]{1,0:T(8,128)(2,1)} async-done(((bf16[24,2304]{1,0:T(8,128)(2,1)}), bf16[768,2304]{1,0:T(8,128)(2,1)}) %all-gather.5.cloned.1.call-update) | async-done | bytes 3538960 | tf_op jit(solution)/shard_map/all_gather | solution.py:82
  72.7 3.2 fusion.1
  78.0 1.7 fusion.71
  80.3 1.6 fusion.30
  81.9 2.3 copy.70
  84.2 44.3 %all-gather.7.cloned.1.call-done = bf16[768,768]{1,0:T(8,128)(2,1)} async-done(((bf16[24,768]{1,0:T(8,128)(2,1)}), bf16[768,768]{1,0:T(8,128)(2,1)}) %all-gather.7.cloned.1.call-update) | async-done | bytes 1179664 | tf_op jit(solution)/shard_map/all_gather | solution.py:84
  128.5 2.1 fusion.72
  132.4 61.6 %all-gather.9.cloned.1.call-done = bf16[768,3072]{1,0:T(8,128)(2,1)} async-done(((bf16[24,3072]{1,0:T(8,128)(2,1)}), bf16[768,3072]{1,0:T(8,128)(2,1)}) %all-gather.9.cloned.1.call-update) | async-done | bytes 4718608 | tf_op jit(solution)/shard_map/all_gather | solution.py:88
  194.0 11.8 %multiply_convert_fusion = (bf16[256,3072]{1,0:T(8,128)(2,1)}, f32[256,3072]{1,0:T(8,128)}, f32[256,3072]{1,0:T(8,128)}) fusion(f32[3072]{0:T(1024)} %convert_element_type.101, bf16[768,3072]{1,0:T(8,128)(2,1)} %all-gather.9.cloned.1.call-done, f32[256,768]{1,0:T(8,128)} %copy-done, f32[768]{0:T(1024)S(1)} %convert_element_type.99, ...), kind=kOutput, calls=%fused_computation.14 | convolution fusion | flops 1260847104 | bytes 13389824 | tf_op jit(solution)/shard_map/dot_general | solution.py:138
  205.8 53.5 %all-gather.11.cloned.1.call-done = bf16[3072,768]{1,0:T(8,128)(2,1)} async-done(((bf16[96,768]{1,0:T(8,128)(2,1)}), bf16[3072,768]{1,0:T(8,128)(2,1)}) %all-gather.11.cloned.1.call-update) | async-done | bytes 4718608 | tf_op jit(solution)/shard_map/all_gather | solution.py:90
  259.3 4.6 fusion.73
  267.1 2.7 convert_reduce_fusion
  269.9 2.3 multiply_reduce_fusion.2
  273.3 2.1 fusion.60
  278.6 3.3 fusion.74
  281.8 1.6 fusion.41
  283.4 4.9 fusion.47
  288.4 5.0 fusion.44
  293.4 7.3 %fusion.61 = f32[768,3072]{1,0:T(8,128)} fusion(bf16[256,3072]{1,0:T(8,128)(2,1)} %copy-done.15, f32[256,768]{1,0:T(8,128)} %copy-done, f32[768]{0:T(1024)S(1)} %convert_element_type.99, f32[768]{0:T(1024)S(1)} %convert_element_type.98, f32[256]{0:T(256)S(1)} %copy-done.32, f32[256]{0:T(256)S(1)} %copy-done.25), kind=kOutput, calls=%fused_computation.107 | convolution fusion | flops 1208942592 | bytes 11804672 | tf_op jit(solution)/shard_map/dot_general | solution.py:39
  300.7 4.0 convolution_bitcast_fusion
  304.7 8.2 %copy.75 = f32[768,2304]{1,0:T(8,128)} copy(f32[768,2304]{0,1:T(8,128)} %convolution_bitcast_fusion) | data formatting | bytes 14155776 | tf_op jit(solution)/shard_map/dot_general | solution.py:39
  312.9 13.5 %pad_maximum_fusion = f32[768,6144]{1,0:T(8,128)} fusion(f32[768,3072]{1,0:T(8,128)} %fusion.61, f32[768,768]{1,0:T(8,128)S(1)} %copy-done.2, f32[768,2304]{1,0:T(8,128)} %copy.75), kind=kLoop, calls=%fused_computation.1 | loop fusion | flops 9437184 | bytes 37748736 | tf_op jit(solution)/shard_map/concatenate | solution.py:219
  326.5 1.3 copy-done.7
  327.9 5.3 fusion.75
  333.9 40.3 %all-reduce.16 = (f32[1536]{0:T(1024)S(1)}, f32[768]{0:T(1024)S(1)}, f32[768]{0:T(1024)S(1)}, f32[768]{0:T(1024)S(1)}, f32[3072]{0:T(1024)S(1)}, /*index=5*/f32[...) all-reduce(f32[1536]{0:T(1024)S(1)} %pad_maximum_fusion.3, ...), channel_id=3, replica_groups=mesh['fsdp'=32] {'fsdp'}, use_global_device_ids=true, to_apply=%region_16.17.clone | all-reduce | flops 9216 | bytes 73728
  378.9 3.9 fusion.39
  382.8 147.6 %reduce-scatter.3.cloned.1.call-done = f32[24,6144]{1,0:T(8,128)} async-done(((f32[768,6144]{1,0:T(8,128)}), f32[24,6144]{1,0:T(8,128)}) %reduce-scatter.3.cloned.1.call-update) | async-done | bytes 589840 | tf_op jit(solution)/shard_map/reduce_scatter | solution.py:218
  530.4 1.5 slice.48
  531.9 1.6 slice.45
  533.6 1.7 slice.49
  535.3 135.3 %reduce-scatter.5.cloned.1.call-done = f32[96,768]{1,0:T(8,128)} async-done(((f32[3072,768]{1,0:T(8,128)}), f32[96,768]{1,0:T(8,128)}) %reduce-scatter.5.cloned.1.call-update) | async-done | bytes 294928 | tf_op jit(solution)/shard_map/reduce_scatter | solution.py:166
  (170 shorter events, 31.6 us)
Async XLA Ops:
  7.2 65.5 %all-gather.5.cloned.1.call-start = ((), (), s32[]{:S(2)}) async-start(), calls=%async_computation.2 | async-start | bytes 3649536 | tf_op jit(solution)/shard_map/all_gather | solution.py:82
  7.9 120.6 %all-gather.7.cloned.1.call-start = ((), (), s32[]{:S(2)}) async-start(), calls=%async_computation.3 | async-start | bytes 1216512 | tf_op jit(solution)/shard_map/all_gather | solution.py:84
  8.7 185.3 %all-gather.9.cloned.1.call-start = ((), (), s32[]{:S(2)}) async-start(), calls=%async_computation.4 | async-start | bytes 4866048 | tf_op jit(solution)/shard_map/all_gather | solution.py:88
  9.4 249.8 %all-gather.11.cloned.1.call-start = ((), (), s32[]{:S(2)}) async-start(), calls=%async_computation.5 | async-start | bytes 4866048 | tf_op jit(solution)/shard_map/all_gather | solution.py:90
  10.0 520.4 %reduce-scatter.3.cloned.1.call-start = ((), (), s32[]{:S(2)}) async-start(), calls=%async_computation.6 | async-start | bytes 19464192 | tf_op jit(solution)/shard_map/reduce_scatter | solution.py:218
  77.1 3.1 copy-start.16
  80.3 48.2 %copy-start.12 = (bf16[256,768]{1,0:T(8,128)(2,1)S(1)}, bf16[256,768]{1,0:T(8,128)(2,1)}, u32[]{:S(2)}) copy-start(bf16[256,768]{1,0:T(8,128)(2,1)} %param.15) | copy-start | bytes 1179652
  128.5 3.3 copy-start.20
  128.5 3.3 copy-start.23
  130.7 141.5 %copy-start.24 = (f32[256]{0:T(256)}, f32[256]{0:T(256)S(1)}, u32[]{:S(2)}) copy-start(f32[256]{0:T(256)S(1)} %broadcast_multiply_fusion.1) | copy-start | bytes 3076
  131.8 140.4 %copy-start.31 = (f32[256]{0:T(256)}, f32[256]{0:T(256)S(1)}, u32[]{:S(2)}) copy-start(f32[256]{0:T(256)S(1)} %fusion.55) | copy-start | bytes 3076
  132.4 126.8 %copy-start.34 = (f32[768]{0:T(1024)S(1)}, f32[768]{0:T(1024)}, u32[]{:S(2)}) copy-start(f32[768]{0:T(1024)} %convert_element_type.103) | copy-start | bytes 9220
  259.2 7.9 %slice-start.2 = ((s8[4718592]{0:T(1024)(128)(4,1)}), s8[4194304]{0:T(1024)(128)(4,1)S(1)}, s32[]{:S(2)}) async-start(s8[4718592]{0:T(1024)(128)(4,1)} %bitcast.68), calls=%async_computation.10 | async-start | bytes 8388608
  259.2 4.9 copy-start.14
  259.2 5.9 copy-start.26
  259.2 7.8 %slice-start.3 = ((s8[4718592]{0:T(1024)(128)(4,1)}), s8[524288]{0:T(1024)(128)(4,1)S(1)}, s32[]{:S(2)}) async-start(s8[4718592]{0:T(1024)(128)(4,1)} %bitcast.68), calls=%async_computation.11 | async-start | bytes 1048576
  259.3 7.8 %copy-start.40 = (f32[256,3072]{1,0:T(8,128)S(1)}, f32[256,3072]{1,0:T(8,128)}, u32[]{:S(2)}) copy-start(f32[256,3072]{1,0:T(8,128)} %get-tuple-element.62) | copy-start | bytes 9437188
  263.9 3.2 copy-start.39
  266.4 3.5 slice-start
  272.2 3.2 copy-start.18
  272.6 2.8 copy-start.5
  272.6 2.8 copy-start.37
  277.8 4.0 copy-start.21
  288.4 5.0 copy-start.25
  288.4 5.0 copy-start.32
  293.4 7.3 %copy-start.10 = (bf16[12,64,256]{2,1,0:T(8,128)(2,1)S(1)}, bf16[12,64,256]{2,1,0:T(8,128)(2,1)}, u32[]{:S(2)}) copy-start(bf16[12,64,256]{2,1,0:T(8,128)(2,1)} %fusion.47) | copy-start | bytes 1179652
  293.4 7.3 %copy-start.11 = (bf16[12,64,256]{2,1,0:T(8,128)(2,1)S(1)}, bf16[12,64,256]{2,1,0:T(8,128)(2,1)}, u32[]{:S(2)}) copy-start(bf16[12,64,256]{2,1,0:T(8,128)(2,1)} %fusion.44) | copy-start | bytes 1179652
  293.4 7.3 %copy-start.13 = (bf16[256,768]{1,0:T(8,128)(2,1)S(1)}, bf16[256,768]{1,0:T(8,128)(2,1)}, u32[]{:S(2)}) copy-start(bf16[256,768]{1,0:T(8,128)(2,1)} %param.15) | copy-start | bytes 1179652
  304.7 8.2 %copy-start.2 = (f32[768,768]{1,0:T(8,128)S(1)}, f32[768,768]{1,0:T(8,128)}, u32[]{:S(2)}) copy-start(f32[768,768]{1,0:T(8,128)} %fusion.60) | copy-start | bytes 7077892
  326.4 344.1 %reduce-scatter.5.cloned.1.call-start = ((), (), s32[]{:S(2)}) async-start(), calls=%async_computation.7 | async-start | bytes 9732096 | tf_op jit(solution)/shard_map/reduce_scatter | solution.py:166
  333.2 45.7 %copy-start.6 = (f32[256,768]{1,0:T(8,128)S(1)}, f32[256,768]{1,0:T(8,128)}, u32[]{:S(2)}) copy-start(f32[256,768]{1,0:T(8,128)} %copy-done.5) | copy-start | bytes 2359300
  333.2 45.7 %copy-start.38 = (f32[256]{0:T(256)S(1)}, f32[256]{0:T(256)}, u32[]{:S(2)}) copy-start(f32[256]{0:T(256)} %copy-done.37) | copy-start | bytes 3076
  (19 other events, 27.1 us)
Sparse Core Ops, SparseCore 0:
  10.9 61.7 all-gather.4
  75.6 52.8 all-gather.6
  131.4 62.5 all-gather.8
  196.7 62.4 all-gather.10
  326.6 203.8 reduce-scatter.2
  536.7 133.7 reduce-scatter.4
where the time goes:
time: 682 us; the launch traced here: 677 us
  waiting for transfers between devices  456 us (67%)
  blocking collectives  80.3 us (12%)
  matrix products  68.6 us (10%)
  local copies, waits for them, and re-layouts  33.4 us (5%)
  other arithmetic  24.3 us (4%)
  between operations  14.6 us (2%)
    reduce_scatter x1, waiting for transfers between devices, shards(): lax.psum_scatter(jnp.concatenate([column_term(hidden, grad_qkv), column_t...  148 us
    reduce_scatter x1, waiting for transfers between devices, shards(): lax.psum_scatter(column_term(gated_low, grad_branch_two), 'fsdp', scatter...  135 us
    unnamed x2, blocking collectives  80.3 us
    all_gather x1, waiting for transfers between devices, shards(): lax.all_gather(w_in, 'fsdp', axis=0, tiled=True)  61.6 us
    all_gather x1, waiting for transfers between devices, shards(): lax.all_gather(w_back, 'fsdp', axis=0, tiled=True)  53.5 us
    all_gather x1, waiting for transfers between devices, shards(): lax.all_gather(w_out, 'fsdp', axis=0, tiled=True)  44.3 us
    dot_general x4, matrix products, outer_sum(): lax.dot_general(left, right, (((0,), (0,)), ((), ())), preferred_element_...  18.6 us
    unnamed x114, local copies, waits for them, and re-layouts  14.8 us
  transfers between devices with their start and end apart: 6, of which 6 were waited for; matrix products, arithmetic and copies ran while one was open for 8% of the time, Pallas kernels for 0%

commit v1 on v0

--- a/solution.py
+++ b/solution.py
@@ -1,12 +1,351 @@
+import functools
+
 import jax
 import jax.numpy as jnp
 from jax import lax
+from jax.experimental import pallas as pl
+from jax.experimental.pallas import tpu as pltpu
 from jax.sharding import PartitionSpec as P
 
 HEAD_DIM = 64
+MESH = pl.DeviceIdType.MESH
+VMEM_LIMIT = 60 * 1024 * 1024
 
 
 EPSILON = 1e-12
+
+
+def chip_grid(count):
+    chips = count // 2
+    side = 1
+    while 2 * side**3 < chips:
+        side += 1
+    if 2 * side**3 == chips:
+        return side, 2 * side
+    return 1, chips
+
+
+class Place:
+    def __init__(self, me, side, depth):
+        self.me, self.side, self.depth = me, side, depth
+        self.core = lax.rem(me, 2)
+        chip = me // 2
+        x, y = lax.rem(chip, side), lax.rem(chip // side, side)
+        self.first = chip // (side * side)
+        self.second = x + self.core * (y - x)
+        self.third = y + self.core * (x - y)
+        self.sibling = me + 1 - 2 * self.core
+
+    def chip(self, de, db, da):
+        return self.chip_for(self.core, self.first, self.second, self.third, de, db, da)
+
+    def sibling_chip(self, de, db, da):
+        return self.chip_for(1 - self.core, self.first, self.third, self.second, de, db, da)
+
+    def chip_for(self, core, first, second, third, de, db, da):
+        side = self.side
+        one = lax.rem(first + de, self.depth)
+        two = lax.rem(second + db, side)
+        three = lax.rem(third + da, side)
+        return (
+            one * (side * side)
+            + two * (1 + core * (side - 1))
+            + three * (side - core * (side - 1))
+        )
+
+    def device(self, de, db, da):
+        return 2 * self.chip(de, db, da) + self.core
+
+    def partners(self):
+        return (
+            [self.device(0, 0, da) for da in range(1, self.side)]
+            + [self.device(0, db, 0) for db in range(1, self.side)]
+            + [self.device(de, 0, 0) for de in range(1, self.depth)]
+            + [self.sibling]
+        )
+
+
+def greet(place):
+    barrier = pltpu.get_barrier_semaphore()
+    partners = place.partners()
+    for partner in partners:
+        pl.semaphore_signal(barrier, inc=1, device_id=(partner,), device_id_type=MESH)
+    pl.semaphore_wait(barrier, len(partners))
+
+
+def gather_kernel(side, depth, src, out, send_sem, recv_sem, own_sem):
+    place = Place(lax.axis_index("fsdp"), side, depth)
+    me, count = place.me, 2 * side * side * depth
+    greet(place)
+    own = pltpu.make_async_copy(src, out.at[me], own_sem)
+    own.start()
+
+    def send(block, slot, device, ticket):
+        pltpu.make_async_remote_copy(
+            src_ref=block,
+            dst_ref=out.at[slot],
+            send_sem=send_sem.at[ticket],
+            recv_sem=recv_sem.at[slot],
+            device_id=(device,),
+            device_id_type=MESH,
+        ).start()
+
+    def arrive(slot):
+        pltpu.make_async_copy(out.at[slot], out.at[slot], recv_sem.at[slot]).wait()
+
+    for ticket, partner in enumerate(place.partners()):
+        send(src, me, partner, ticket)
+    base = 2 * (side - 1) + depth
+    per_depth = side * side + side - 1
+
+    def near(de, db, ticket):
+        slot = place.device(de, db, 0)
+        arrive(slot)
+        for da in range(1, side):
+            send(out.at[slot], slot, place.device(0, 0, da), ticket + da - 1)
+        ticket = ticket + side - 1
+        if db == 0:
+            for other in range(1, side):
+                send(out.at[slot], slot, place.device(0, other, 0), ticket + other - 1)
+            ticket = ticket + side - 1
+        send(out.at[slot], slot, place.sibling, ticket)
+        return ticket + 1
+
+    def far(de, ticket):
+        for da in range(1, side):
+            for db in range(side):
+                slot = place.device(de, db, da)
+                arrive(slot)
+                send(out.at[slot], slot, place.sibling, ticket)
+                ticket = ticket + 1
+        return ticket
+
+    ticket = base
+    for db in range(1, side):
+        ticket = near(0, db, ticket)
+    start = ticket
+
+    def step(de, carry):
+        ticket = start + (de - 1) * (2 * side * side - 1)
+        for db in range(side):
+            ticket = near(de, db, ticket)
+        far(de - 1, ticket)
+        return carry
+
+    lax.fori_loop(1, depth, step, 0)
+    far(depth - 1, count - 1 - side * (side - 1))
+
+    def from_sibling(chip, carry):
+        arrive(2 * chip + 1 - place.core)
+        return carry
+
+    lax.fori_loop(0, count // 2, from_sibling, 0)
+    own.wait()
+
+    def sent(ticket, carry):
+        pltpu.make_async_copy(src, src, send_sem.at[ticket]).wait()
+        return carry
+
+    lax.fori_loop(0, count - 1, sent, 0)
+
+
+def gather_blocks(block, count):
+    side, depth = chip_grid(count)
+    return pl.pallas_call(
+        functools.partial(gather_kernel, side, depth),
+        out_shape=jax.ShapeDtypeStruct((count,) + block.shape, block.dtype),
+        in_specs=[pl.BlockSpec(memory_space=pl.ANY)],
+        out_specs=pl.BlockSpec(memory_space=pl.ANY),
+        scratch_shapes=[
+            pltpu.SemaphoreType.DMA((count,)),
+            pltpu.SemaphoreType.DMA((count,)),
+            pltpu.SemaphoreType.DMA,
+        ],
+        compiler_params=pltpu.CompilerParams(
+            collective_id=0, has_side_effects=True, vmem_limit_bytes=VMEM_LIMIT
+        ),
+    )(block)
+
+
+def scatter_kernel(
+    side, depth, terms, out, pair, third, second, first, send_sem, pair_sem, third_sem, second_sem, first_sem
+):
+    place = Place(lax.axis_index("fsdp"), side, depth)
+    core, chips = place.core, side * side * depth
+    count = 2 * chips
+    greet(place)
+
+    def send(block, target, sem, device, ticket):
+        pltpu.make_async_remote_copy(
+            src_ref=block,
+            dst_ref=target,
+            send_sem=send_sem.at[ticket],
+            recv_sem=sem,
+            device_id=(device,),
+            device_id_type=MESH,
+        ).start()
+
+    def arrive(block, sem):
+        pltpu.make_async_copy(block, block, sem).wait()
+
+    def wide(block):
+        return block[...].astype(jnp.float32)
+
+    def give(index, carry):
+        da = lax.rem(index // (side * depth) + 1, side)
+        de = lax.rem(lax.rem(index, side * depth) // side + 1, depth)
+        db = lax.rem(lax.rem(index, side) + 1, side)
+        chip = place.sibling_chip(de, db, da)
+        send(terms.at[2 * chip + 1 - core], pair.at[chip], pair_sem.at[chip], place.sibling, chip)
+        return carry
+
+    lax.fori_loop(0, chips, give, 0)
+
+    def outward(index, carry):
+        da = index // (side * depth) + 1
+        de = lax.rem(lax.rem(index, side * depth) // side + 1, depth)
+        db = lax.rem(lax.rem(index, side) + 1, side)
+        chip = place.chip(de, db, da)
+        held = pair.at[chip]
+        arrive(held, pair_sem.at[chip])
+        held[...] = (wide(held) + wide(terms.at[2 * chip + core])).astype(held.dtype)
+        slot = de * side + db
+        send(
+            held,
+            third.at[side - 1 - da, slot],
+            third_sem.at[side - 1 - da, slot],
+            place.device(0, 0, da),
+            chips + index,
+        )
+        return carry
+
+    lax.fori_loop(0, chips - side * depth, outward, 0)
+    base = 2 * chips - side * depth
+
+    def along_second(de, ticket):
+        for db in list(range(1, side)) + [0]:
+            chip = place.chip(de, db, 0)
+            held = pair.at[chip]
+            arrive(held, pair_sem.at[chip])
+            slot = de * side + db
+            total = wide(held) + wide(terms.at[2 * chip + core])
+            for other in range(side - 1):
+                arrive(third.at[other, slot], third_sem.at[other, slot])
+                total = total + wide(third.at[other, slot])
+            held[...] = total.astype(held.dtype)
+            if db > 0:
+                send(
+                    held,
+                    second.at[side - 1 - db, de],
+                    second_sem.at[side - 1 - db, de],
+                    place.device(0, db, 0),
+                    ticket + db - 1,
+                )
+
+    def second_total(de):
+        held = pair.at[place.chip(de, 0, 0)]
+        total = wide(held)
+        for other in range(side - 1):
+            arrive(second.at[other, de], second_sem.at[other, de])
+            total = total + wide(second.at[other, de])
+        return held, total
+
+    def along_first(de):
+        held, total = second_total(de)
+        held[...] = total.astype(held.dtype)
+        send(
+            held,
+            first.at[depth - 1 - de],
+            first_sem.at[depth - 1 - de],
+            place.device(de, 0, 0),
+            count - 1 - de,
+        )
+
+    def step(index, carry):
+        along_second(lax.rem(index, depth), base + (index - 1) * (side - 1))
+
+        @pl.when(index > 1)
+        def last():
+            along_first(index - 1)
+
+        return carry
+
+    lax.fori_loop(1, depth + 1, step, 0)
+    held, total = second_total(0)
+    for other in range(depth - 1):
+        arrive(first.at[other], first_sem.at[other])
+        total = total + wide(first.at[other])
+    out[...] = total
+
+    def sent(ticket, carry):
+        pltpu.make_async_copy(terms.at[0], terms.at[0], send_sem.at[ticket]).wait()
+        return carry
+
+    lax.fori_loop(0, count - 1, sent, 0)
+
+
+def scatter_blocks(terms):
+    count = terms.shape[0]
+    side, depth = chip_grid(count)
+    block = terms.shape[1:]
+    chips = count // 2
+    lanes = max(side - 1, 1)
+    return pl.pallas_call(
+        functools.partial(scatter_kernel, side, depth),
+        out_shape=jax.ShapeDtypeStruct(block, jnp.float32),
+        in_specs=[pl.BlockSpec(memory_space=pltpu.VMEM)],
+        out_specs=pl.BlockSpec(memory_space=pltpu.VMEM),
+        scratch_shapes=[
+            pltpu.VMEM((chips,) + block, terms.dtype),
+            pltpu.VMEM((lanes, side * depth) + block, terms.dtype),
+            pltpu.VMEM((lanes, depth) + block, terms.dtype),
+            pltpu.VMEM((depth - 1,) + block, terms.dtype),
+            pltpu.SemaphoreType.DMA((count,)),
+            pltpu.SemaphoreType.DMA((chips,)),
+            pltpu.SemaphoreType.DMA((lanes, side * depth)),
+            pltpu.SemaphoreType.DMA((lanes, depth)),
+            pltpu.SemaphoreType.DMA((depth - 1,)),
+        ],
+        compiler_params=pltpu.CompilerParams(
+            collective_id=1, has_side_effects=True, vmem_limit_bytes=VMEM_LIMIT
+        ),
+    )(terms)
+
+
+def padded_rows(rows):
+    return -(-rows // 16) * 16
+
+
+def chunk_columns(weight, width):
+    return jnp.concatenate(
+        [weight[:, :, start : start + width] for start in range(0, weight.shape[2], width)], axis=1
+    )
+
+
+def pack(matrices, vectors, width, dtype):
+    parts = [chunk_columns(matrix.astype(dtype), width) for matrix in matrices]
+    line = jnp.concatenate([vector.astype(dtype) for vector in vectors], axis=1)
+    rows = sum(part.shape[1] for part in parts)
+    tail = padded_rows(rows + -(-line.shape[1] // width)) - rows
+    line = jnp.pad(line, ((0, 0), (0, tail * width - line.shape[1])))
+    return jnp.concatenate(parts + [line.reshape(line.shape[0], tail, width)], axis=1)
+
+
+def unpack(blocks, matrix_shapes, vector_sizes):
+    count, _, width = blocks.shape
+    matrices, row = [], 0
+    for rows, columns in matrix_shapes:
+        chunks = []
+        for _ in range(columns // width):
+            chunks.append(blocks[:, row : row + rows, :].reshape(count * rows, width))
+            row += rows
+        matrices.append(jnp.concatenate(chunks, axis=1))
+    line = blocks[:, row:, :].reshape(count, -1)
+    vectors, place = [], 0
+    for size in vector_sizes:
+        vectors.append(line[:, place : place + size].reshape(count * size))
+        place += size
+    return matrices, vectors
 
 
 def layer_norm(values, gain, shift):
@@ -78,34 +417,30 @@
     factor = HEAD_DIM ** (-0.5)
     alive_row, same_seq = seq_masks(seq_lengths, row_count)
     alive_col = alive_row.astype(jnp.float32)[:, None]
-    gathered = (
-        lax.all_gather(w_qkv, "fsdp", axis=0, tiled=True),
-        lax.all_gather(b_qv, "fsdp", axis=0, tiled=True),
-        lax.all_gather(w_out, "fsdp", axis=0, tiled=True),
-        lax.all_gather(b_out, "fsdp", axis=0, tiled=True),
-        lax.all_gather(gain_one, "fsdp", axis=0, tiled=True),
-        lax.all_gather(shift_one, "fsdp", axis=0, tiled=True),
-        lax.all_gather(w_in, "fsdp", axis=0, tiled=True),
-        lax.all_gather(b_in, "fsdp", axis=0, tiled=True),
-        lax.all_gather(w_back, "fsdp", axis=0, tiled=True),
-        lax.all_gather(b_back, "fsdp", axis=0, tiled=True),
-        lax.all_gather(gain_two, "fsdp", axis=0, tiled=True),
-        lax.all_gather(shift_two, "fsdp", axis=0, tiled=True),
+    count = lax.axis_size("fsdp")
+    weights = (w_qkv, w_out, w_in, w_back)
+    biases = (b_qv, b_out, gain_one, shift_one, b_in, b_back, gain_two, shift_two)
+    weight_shapes = [weight.shape for weight in weights]
+    bias_sizes = [bias.shape[0] for bias in biases]
+    block = pack(
+        [weight[None] for weight in weights],
+        [bias[None] for bias in biases],
+        model_width,
+        jnp.bfloat16,
+    )[0]
+    (full_qkv, full_out, full_in, full_back), full_biases = unpack(
+        gather_blocks(block, count), weight_shapes, bias_sizes
     )
     (
-        full_qkv,
         full_bqv,
-        full_out,
         full_bout,
         full_gone,
         full_sone,
-        full_in,
         full_bin,
-        full_back,
         full_bback,
         full_gtwo,
         full_stwo,
-    ) = gathered
+    ) = full_biases
     bias_qv = full_bqv.astype(jnp.float32)
     bias_qkv = jnp.concatenate(
         [bias_qv[:model_width], jnp.zeros((model_width,), jnp.float32), bias_qv[model_width:]]
@@ -148,38 +483,26 @@
         layer_norm(summed_two, full_gtwo.astype(jnp.float32), full_stwo.astype(jnp.float32))
         * alive_col
     ).astype(jnp.bfloat16)
-    again = (
-        lax.all_gather(w_qkv, "fsdp", axis=0, tiled=True),
-        lax.all_gather(w_out, "fsdp", axis=0, tiled=True),
-        lax.all_gather(w_in, "fsdp", axis=0, tiled=True),
-        lax.all_gather(w_back, "fsdp", axis=0, tiled=True),
-        lax.all_gather(gain_one, "fsdp", axis=0, tiled=True),
-        lax.all_gather(gain_two, "fsdp", axis=0, tiled=True),
-    )
-    back_qkv, back_out, back_in, back_back, back_gone, back_gtwo = again
     shift_zero = jnp.zeros((model_width,), jnp.float32)
     unused, norm_two_back = jax.vjp(
-        layer_norm, summed_two, back_gtwo.astype(jnp.float32), shift_zero
+        layer_norm, summed_two, full_gtwo.astype(jnp.float32), shift_zero
     )
     grad_sum_two, grad_gtwo, grad_stwo = norm_two_back(cotangent.astype(jnp.float32) * alive_col)
     grad_branch_two = grad_sum_two.astype(jnp.bfloat16)
-    share_back = lax.psum_scatter(
-        column_term(gated_low, grad_branch_two), "fsdp", scatter_dimension=0, tiled=True
-    )
     term_bback = jnp.sum(grad_branch_two.astype(jnp.float32), axis=0)
-    grad_gated = back_product(grad_branch_two, back_back)
+    grad_gated = back_product(grad_branch_two, full_back)
     unused, gate_back = jax.vjp(smooth_gate, inner)
     grad_inner = gate_back(grad_gated)[0].astype(jnp.bfloat16)
     term_bin = jnp.sum(grad_inner.astype(jnp.float32), axis=0)
-    grad_normed = grad_sum_two + back_product(grad_inner, back_in)
+    grad_normed = grad_sum_two + back_product(grad_inner, full_in)
     unused, norm_one_back = jax.vjp(
-        layer_norm, summed_one, back_gone.astype(jnp.float32), shift_zero
+        layer_norm, summed_one, full_gone.astype(jnp.float32), shift_zero
     )
     grad_sum_one, grad_gone, grad_sone = norm_one_back(grad_normed)
     grad_branch_one = grad_sum_one.astype(jnp.bfloat16)
     term_bout = jnp.sum(grad_branch_one.astype(jnp.float32), axis=0)
     grad_attended = (
-        (back_product(grad_branch_one, back_out) * alive_col)
+        (back_product(grad_branch_one, full_out) * alive_col)
         .astype(jnp.bfloat16)
         .reshape(row_count, head_count, HEAD_DIM)
     )
@@ -214,32 +537,35 @@
     ).astype(jnp.bfloat16)
     column_sums = jnp.sum(grad_qkv.astype(jnp.float32), axis=0)
     term_bqv = jnp.concatenate([column_sums[:model_width], column_sums[2 * model_width :]])
-    grad_hidden = (grad_sum_one + back_product(grad_qkv, back_qkv)).astype(jnp.bfloat16)
-    share_all = lax.psum_scatter(
-        jnp.concatenate(
-            [
-                column_term(hidden, grad_qkv),
-                column_term(attended_low, grad_branch_one),
-                column_term(normed_low, grad_inner),
-            ],
-            axis=1,
-        ),
-        "fsdp",
-        scatter_dimension=0,
-        tiled=True,
-    )
-    share_qkv = share_all[:, : 3 * model_width]
-    share_out = share_all[:, 3 * model_width : 4 * model_width]
-    share_in = share_all[:, 4 * model_width :]
-    vectors = (
-        lax.psum_scatter(term_bqv, "fsdp", scatter_dimension=0, tiled=True),
-        lax.psum_scatter(term_bout, "fsdp", scatter_dimension=0, tiled=True),
-        lax.psum_scatter(grad_gone, "fsdp", scatter_dimension=0, tiled=True),
-        lax.psum_scatter(grad_sone, "fsdp", scatter_dimension=0, tiled=True),
-        lax.psum_scatter(term_bin, "fsdp", scatter_dimension=0, tiled=True),
-        lax.psum_scatter(term_bback, "fsdp", scatter_dimension=0, tiled=True),
-        lax.psum_scatter(grad_gtwo, "fsdp", scatter_dimension=0, tiled=True),
-        lax.psum_scatter(grad_stwo, "fsdp", scatter_dimension=0, tiled=True),
+    grad_hidden = (grad_sum_one + back_product(grad_qkv, full_qkv)).astype(jnp.bfloat16)
+    terms = pack(
+        [
+            column_term(left, right).reshape(count, -1, right.shape[1])
+            for left, right in (
+                (hidden, grad_qkv),
+                (attended_low, grad_branch_one),
+                (normed_low, grad_inner),
+                (gated_low, grad_branch_two),
+            )
+        ],
+        [
+            vector.reshape(count, -1)
+            for vector in (
+                term_bqv,
+                term_bout,
+                grad_gone,
+                grad_sone,
+                term_bin,
+                term_bback,
+                grad_gtwo,
+                grad_stwo,
+            )
+        ],
+        model_width,
+        jnp.bfloat16,
+    )
+    (share_qkv, share_out, share_in, share_back), vectors = unpack(
+        scatter_blocks(terms)[None], weight_shapes, bias_sizes
     )
     return (
         output,

time: 682 us -> 312 us (0.46)
  waiting for transfers between devices: 456 us -> 0 us
  Pallas kernels: 0 us -> 184 us
  blocking collectives: 80.3 us -> 0 us
  local copies, waits for them, and re-layouts: 33.4 us -> 52.1 us
  between operations: 14.6 us -> 1.41 us
  matrix products: 68.6 us -> 56.8 us
  other arithmetic: 24.3 us -> 16.5 us
    reduce_scatter x2 -> x0, waiting for transfers between devices: 283 us -> none  [the longest x1 148 us: shards(): lax.psum_scatter(jnp.concatenate([column_term(hidden, grad_qkv), column_t...]
    pallas_call x0 -> x2, Pallas kernels: none -> 184 us  [the longest x1 105 us: scatter_blocks(): pl.pallas_call(functools.partial(scatter_kernel, side, depth), out_shape=...]
    all_gather x4 -> x0, waiting for transfers between devices: 170 us -> none  [the longest x1 61.6 us: shards(): lax.all_gather(w_in, 'fsdp', axis=0, tiled=True)]
    unnamed x2 -> x0, blocking collectives: 80.3 us -> none
    concatenate x1 -> x2, other arithmetic: 13.5 us -> 1.43 us  [unpack(): matrices.append(jnp.concatenate(chunks, axis=1))]
    dot_general x4, matrix products: 18.6 us -> 7.08 us  [outer_sum(): lax.dot_general(left, right, (((0,), (0,)), ((), ())), preferred_element_...]
    unnamed x114 -> x135, local copies, waits for them, and re-layouts: 14.8 us -> 23 us
    dot_general x1, local copies, waits for them, and re-layouts: 8.19 us -> 0.17 us  [outer_sum(): lax.dot_general(left, right, (((0,), (0,)), ((), ())), preferred_element_...]
  transfers between devices with their start and end apart: 6 -> 0, of which waited for: 6 -> 0; matrix products, arithmetic and copies ran while one was open for 8% -> 0% of each run, Pallas kernels for 0% -> 0%
where the time goes in v1:
time: 312 us; the launch traced here: 310 us
  Pallas kernels  184 us (59%)
  matrix products  56.8 us (18%)
  local copies, waits for them, and re-layouts  52.1 us (17%)
  other arithmetic  16.5 us (5%)
    pallas_call x1, Pallas kernels, scatter_blocks(): pl.pallas_call(functools.partial(scatter_kernel, side, depth), out_shape=...  105 us
    pallas_call x1, Pallas kernels, gather_blocks(): pl.pallas_call(functools.partial(gather_kernel, side, depth), out_shape=j...  78.9 us
    unnamed x135, local copies, waits for them, and re-layouts  23 us
    dot_general x4, matrix products, back_product(): lax.dot_general(grad, weight, (((1,), (1,)), ((), ())), preferred_element...  14.5 us
    dot_general x1, matrix products, shards(): jnp.dot(normed_low, full_in, preferred_element_type=jnp.float32)  13.8 us
    slice x2, local copies, waits for them, and re-layouts, unpack(): chunks.append(blocks[:, row:row + rows, :].reshape(count * rows, width))  9.98 us
    dot_general x4, matrix products, outer_sum(): lax.dot_general(left, right, (((0,), (0,)), ((), ())), preferred_element_...  7.08 us

profile of v1, /device:TPU:3, one launch (start us, length us, event | category | flops | bytes accessed | tf_op | source)
XLA Modules:
  0.0 310.5 jit_solution(13572298521108545259)
XLA Ops:
  9.5 78.9 %shard_map.254 = bf16[32,304,768]{2,1,0:T(8,128)(2,1)} custom-call(bf16[304,768]{1,0:T(8,128)(2,1)} %bitcast.173), custom_call_target="tpu_custom_call" | custom-call | tf_op jit(solution)/shard_map/pallas_call | solution.py:154
  88.4 1.2 slice.203
  92.0 6.7 %fusion.81 = (bf16[32,24,768]{2,1,0:T(8,128)(2,1)}, bf16[32,24,768]{2,1,0:T(8,128)(2,1)}, bf16[32,24,768]{2,1,0:T(8,128)(2,1)}, bf16[32,24,768]{2,1,0:T(8,128)(2...) fusion(bf16[32,304,768]{2,1,0:T(8,128)(2,1)} %shard_map.254), kind=kLoop, calls=%fused_computation.172 | loop fusion | bytes 18874368 | tf_op jit(solution)/shard_map/slice | solution.py:340
  101.4 2.6 fusion.2
  106.1 1.6 fusion.54
  107.7 1.4 fusion.86
  110.7 1.4 multiply_reduce_fusion.6
  112.6 13.8 %multiply_convert_fusion = (bf16[256,3072]{1,0:T(8,128)(2,1)S(1)}, f32[256,3072]{1,0:T(8,128)}, f32[256,3072]{1,0:T(8,128)}) fusion(f32[3072]{0:T(1024)} %reshape.496, bf16[768,768]{1,0:T(8,128)(2,1)} %bitcast.161, bf16[768,768]{1,0:T(8,128)(2,1)} %bitcast.163, bf16[768,768]{1,0:T(8,128)(2,1)} %bitcast.165, bf16[768,768]{1,0:T(8,128)(2,1)} %bitcast.167, ...), kind=kOutput, calls=%fused_computation.17 | convolution fusion | flops 1279721472 | bytes 13389824 | tf_op jit(solution)/shard_map/dot_general | solution.py:473
  126.5 3.2 %slice.221 = bf16[32,96,768]{2,1,0:T(8,128)(2,1)S(1)} slice(bf16[32,304,768]{2,1,0:T(8,128)(2,1)} %shard_map.254), slice={[0:32], [192:288], [0:768]} | slice | bytes 9437184 | tf_op jit(solution)/shard_map/slice | solution.py:340
  129.8 1.5 fusion.87
  134.4 2.3 copy.49
  136.7 3.1 multiply_reduce_fusion.1
  139.8 1.2 multiply_multiply_fusion.6
  141.0 1.4 reshape.499
  142.4 2.5 fusion.78
  145.6 6.3 %fusion.75 = (bf16[3072]{0:T(1024)(128)(2,1)}, bf16[256,3072]{1,0:T(8,128)(2,1)S(1)}) fusion(f32[256,3072]{1,0:T(8,128)S(1)} %copy-done.56, f32[256,3072]{1,0:T(8,128)} %get-tuple-element.77, bf16[256,768]{1,0:T(8,128)(2,1)S(1)} %get-tuple-element.21, bf16[3072,768]{1,0:T(8,128)(2,1)} %bitcast.133), kind=kOutput, calls=%fused_computation.167 | convolution fusion | flops 1219752960 | bytes 12982272 | tf_op jit(solution)/shard_map/dot_general | solution.py:388
  152.0 2.2 multiply_reduce_fusion.2
  156.1 1.3 fusion.44
  157.4 1.2 copy.45
  159.4 1.4 fusion.45
  160.7 2.3 fusion.88
  163.0 5.0 %fusion.48 = bf16[12,64,256]{2,1,0:T(8,128)(2,1)} fusion(bf16[256,12,64]{0,2,1:T(8,128)(2,1)} %bitcast.149, f32[12,256,256]{1,2,0:T(8,128)} %fusion.88, f32[12,256,256]{1,2,0:T(8,128)S(1)} %get-tuple-element.72, f32[12,256]{1,0:T(8,128)} %copy-done.37, pred[256,256]{0,1:T(8,128)(4,1)} %copy-done.34), kind=kOutput, calls=%fused_computation.62 | convolution fusion | flops 106564864 | bytes 7155712 | tf_op jit(solution)/shard_map/hqk,qhd->khd/dot_general | solution.py:524
  168.0 4.9 %fusion.51 = bf16[12,64,256]{2,1,0:T(8,128)(2,1)} fusion(bf16[256,12,64]{0,2,1:T(8,128)(2,1)S(1)} %bitcast.147, f32[12,256,256]{1,2,0:T(8,128)} %fusion.88, f32[12,256,256]{1,2,0:T(8,128)S(1)} %get-tuple-element.72, f32[12,256]{1,0:T(8,128)} %copy-done.37, pred[256,256]{0,1:T(8,128)(4,1)} %copy-done.34), kind=kOutput, calls=%fused_computation.63 | convolution fusion | flops 106564864 | bytes 7155712 | tf_op jit(solution)/shard_map/hqk,khd->qhd/dot_general | solution.py:520
  173.0 4.8 %fusion.43 = bf16[256,768]{1,0:T(8,128)(2,1)} fusion(bf16[768,768]{1,0:T(8,128)(2,1)} %bitcast.156, bf16[768,768]{1,0:T(8,128)(2,1)} %bitcast.158, bf16[768,768]{1,0:T(8,128)(2,1)} %bitcast.160, f32[256,768]{1,0:T(8,128)} %copy-done.9, f32[256]{0:T(256)} %copy-done.53, bf16[256,768]{0,1:T(8,128)(2,1)} %bitcast.152, bf16[256,768]{0,1:T(8,128)(2,1)} %bitcast.175, ...), kind=kOutput, calls=%fused_computation.59 | convolution fusion | flops 920715264 | bytes 5899264 | tf_op jit(solution)/shard_map/dot_general | solution.py:388
  182.5 1.5 fusion.32
  184.0 3.0 convolution_convert_fusion.1
  187.0 1.2 slice_dynamic-update-slice_fusion.3
  191.5 1.4 convolution_convert_fusion
  193.1 2.5 constant_dynamic-update-slice_fusion.10
  198.1 104.9 %shard_map.255 = f32[304,768]{1,0:T(8,128)} custom-call(bf16[32,304,768]{2,1,0:T(8,128)(2,1)} %constant_dynamic-update-slice_fusion.9.terms), custom_call_target="tpu_custom_call" | custom-call | tf_op jit(solution)/shard_map/pallas_call | solution.py:293
  303.0 1.8 slice_bitcast_fusion.4
  308.8 1.7 slice_bitcast_fusion
  (195 shorter events, 39.1 us)
Async XLA Ops:
  92.0 9.4 %copy-start.30 = (bf16[256,768]{1,0:T(8,128)(2,1)S(1)}, bf16[256,768]{1,0:T(8,128)(2,1)}, u32[]{:S(2)}) copy-start(bf16[256,768]{1,0:T(8,128)(2,1)} %param.15) | copy-start | bytes 1179652
  98.7 5.3 %copy-start.23 = (bf16[32,24,768]{2,1,0:T(8,128)(2,1)}, bf16[32,24,768]{2,1,0:T(8,128)(2,1)S(1)}, u32[]{:S(2)}) copy-start(bf16[32,24,768]{2,1,0:T(8,128)(2,1)S(1)} %get-tuple-element.39) | copy-start | bytes 3538948
  98.7 5.3 %copy-start.24 = (bf16[32,24,768]{2,1,0:T(8,128)(2,1)}, bf16[32,24,768]{2,1,0:T(8,128)(2,1)S(1)}, u32[]{:S(2)}) copy-start(bf16[32,24,768]{2,1,0:T(8,128)(2,1)S(1)} %get-tuple-element.40) | copy-start | bytes 3538948
  101.2 4.8 %copy-start.42 = (f32[256]{0:T(256)}, f32[256]{0:T(256)S(1)}, u32[]{:S(2)}) copy-start(f32[256]{0:T(256)S(1)} %get-tuple-element.32) | copy-start | bytes 3076
  112.6 17.1 %copy-start.40 = (f32[256]{0:T(256)}, f32[256]{0:T(256)S(1)}, u32[]{:S(2)}) copy-start(f32[256]{0:T(256)S(1)} %fusion.62) | copy-start | bytes 3076
  126.5 3.3 %copy-start.7 = (bf16[256,3072]{1,0:T(8,128)(2,1)}, bf16[256,3072]{1,0:T(8,128)(2,1)S(1)}, u32[]{:S(2)}) copy-start(bf16[256,3072]{1,0:T(8,128)(2,1)S(1)} %get-tuple-element.30) | copy-start | bytes 4718596
  126.5 3.3 %copy-start = (f32[256,768]{1,0:T(8,128)S(1)}, f32[256,768]{1,0:T(8,128)}, u32[]{:S(2)}) copy-start(f32[256,768]{1,0:T(8,128)} %get-tuple-element.76) | copy-start | bytes 2359300
  126.5 3.3 %copy-start.52 = (f32[768]{0:T(1024)S(1)}, f32[768]{0:T(1024)}, u32[]{:S(2)}) copy-start(f32[768]{0:T(1024)} %reshape.497) | copy-start | bytes 9220
  129.8 6.9 %copy-start.13 = (bf16[256,768]{1,0:T(8,128)(2,1)S(1)}, bf16[256,768]{1,0:T(8,128)(2,1)}, u32[]{:S(2)}) copy-start(bf16[256,768]{1,0:T(8,128)(2,1)} %param.16) | copy-start | bytes 1179652
  142.4 3.2 %copy-start.56 = (f32[256,3072]{1,0:T(8,128)S(1)}, f32[256,3072]{1,0:T(8,128)}, u32[]{:S(2)}) copy-start(f32[256,3072]{1,0:T(8,128)} %get-tuple-element.31) | copy-start | bytes 9437188
  145.6 6.3 %copy-start.10 = (bf16[256,768]{1,0:T(8,128)(2,1)}, bf16[256,768]{1,0:T(8,128)(2,1)S(1)}, u32[]{:S(2)}) copy-start(bf16[256,768]{1,0:T(8,128)(2,1)S(1)} %get-tuple-element.21) | copy-start | bytes 1179652
  145.6 6.3 %copy-start.1 = (f32[256,768]{1,0:T(8,128)S(1)}, f32[256,768]{1,0:T(8,128)}, u32[]{:S(2)}) copy-start(f32[256,768]{1,0:T(8,128)} %get-tuple-element.76) | copy-start | bytes 2359300
  145.6 6.3 %copy-start.25 = (bf16[32,24,768]{2,1,0:T(8,128)(2,1)S(1)}, bf16[32,24,768]{2,1,0:T(8,128)(2,1)}, u32[]{:S(2)}) copy-start(bf16[32,24,768]{2,1,0:T(8,128)(2,1)} %get-tuple-element.35) | copy-start | bytes 3538948
  145.6 6.3 %copy-start.26 = (bf16[32,24,768]{2,1,0:T(8,128)(2,1)S(1)}, bf16[32,24,768]{2,1,0:T(8,128)(2,1)}, u32[]{:S(2)}) copy-start(bf16[32,24,768]{2,1,0:T(8,128)(2,1)} %get-tuple-element.36) | copy-start | bytes 3538948
  145.6 6.3 %copy-start.27 = (bf16[32,24,768]{2,1,0:T(8,128)(2,1)S(1)}, bf16[32,24,768]{2,1,0:T(8,128)(2,1)}, u32[]{:S(2)}) copy-start(bf16[32,24,768]{2,1,0:T(8,128)(2,1)} %get-tuple-element.37) | copy-start | bytes 3538948
  145.6 6.3 %copy-start.28 = (bf16[32,24,768]{2,1,0:T(8,128)(2,1)S(1)}, bf16[32,24,768]{2,1,0:T(8,128)(2,1)}, u32[]{:S(2)}) copy-start(bf16[32,24,768]{2,1,0:T(8,128)(2,1)} %get-tuple-element.38) | copy-start | bytes 3538948
  145.6 6.3 %copy-start.41 = (f32[256]{0:T(256)S(1)}, f32[256]{0:T(256)}, u32[]{:S(2)}) copy-start(f32[256]{0:T(256)} %copy-done.40) | copy-start | bytes 3076
  163.0 5.0 %copy-start.18 = (bf16[256,768]{0,1:T(8,128)(2,1)S(1)}, bf16[256,768]{0,1:T(8,128)(2,1)}, u32[]{:S(2)}) copy-start(bf16[256,768]{0,1:T(8,128)(2,1)} %copy-done.17) | copy-start | bytes 1179652
  173.0 4.8 %copy-start.22 = (bf16[12,64,256]{2,1,0:T(8,128)(2,1)S(1)}, bf16[12,64,256]{2,1,0:T(8,128)(2,1)}, u32[]{:S(2)}) copy-start(bf16[12,64,256]{2,1,0:T(8,128)(2,1)} %fusion.45) | copy-start | bytes 1179652
  173.0 4.8 %copy-start.31 = (bf16[256,768]{1,0:T(8,128)(2,1)S(1)}, bf16[256,768]{1,0:T(8,128)(2,1)}, u32[]{:S(2)}) copy-start(bf16[256,768]{1,0:T(8,128)(2,1)} %param.15) | copy-start | bytes 1179652
  173.0 4.8 %copy-start.32 = (bf16[12,64,256]{2,1,0:T(8,128)(2,1)S(1)}, bf16[12,64,256]{2,1,0:T(8,128)(2,1)}, u32[]{:S(2)}) copy-start(bf16[12,64,256]{2,1,0:T(8,128)(2,1)} %fusion.48) | copy-start | bytes 1179652
  173.0 4.8 %copy-start.33 = (bf16[12,64,256]{2,1,0:T(8,128)(2,1)S(1)}, bf16[12,64,256]{2,1,0:T(8,128)(2,1)}, u32[]{:S(2)}) copy-start(bf16[12,64,256]{2,1,0:T(8,128)(2,1)} %fusion.51) | copy-start | bytes 1179652
  178.9 3.4 %copy-start.12 = (bf16[768,256]{0,1:T(8,128)(2,1)S(1)}, bf16[768,256]{0,1:T(8,128)(2,1)}, u32[]{:S(2)}) copy-start(bf16[768,256]{0,1:T(8,128)(2,1)} %get-tuple-element.70) | copy-start | bytes 1179652
  188.1 3.4 %copy-start.8 = (bf16[256,3072]{1,0:T(8,128)(2,1)S(1)}, bf16[256,3072]{1,0:T(8,128)(2,1)}, u32[]{:S(2)}) copy-start(bf16[256,3072]{1,0:T(8,128)(2,1)} %copy-done.7) | copy-start | bytes 4718596
  188.1 3.4 %copy-start.11 = (bf16[256,768]{1,0:T(8,128)(2,1)S(1)}, bf16[256,768]{1,0:T(8,128)(2,1)}, u32[]{:S(2)}) copy-start(bf16[256,768]{1,0:T(8,128)(2,1)} %copy-done.10) | copy-start | bytes 1179652
  193.0 3.1 %copy-start.50 = (bf16[768]{0:T(1024)(128)(2,1)S(1)}, bf16[768]{0:T(1024)(128)(2,1)}, u32[]{:S(2)}) copy-start(bf16[768]{0:T(1024)(128)(2,1)} %get-tuple-element.24) | copy-start | bytes 4612
  193.0 3.2 %copy-start.55 = (bf16[768]{0:T(1024)(128)(2,1)S(1)}, bf16[768]{0:T(1024)(128)(2,1)}, u32[]{:S(2)}) copy-start(bf16[768]{0:T(1024)(128)(2,1)} %get-tuple-element.14) | copy-start | bytes 4612
  193.0 3.3 %copy-start.54 = (bf16[768]{0:T(1024)(128)(2,1)S(1)}, bf16[768]{0:T(1024)(128)(2,1)}, u32[]{:S(2)}) copy-start(bf16[768]{0:T(1024)(128)(2,1)} %get-tuple-element.18) | copy-start | bytes 4612
  193.0 3.4 %copy-start.51 = (bf16[3072]{0:T(1024)(128)(2,1)S(1)}, bf16[3072]{0:T(1024)(128)(2,1)}, u32[]{:S(2)}) copy-start(bf16[3072]{0:T(1024)(128)(2,1)} %get-tuple-element.22) | copy-start | bytes 18436
  193.0 3.5 %copy-start.49 = (bf16[768]{0:T(1024)(128)(2,1)S(1)}, bf16[768]{0:T(1024)(128)(2,1)}, u32[]{:S(2)}) copy-start(bf16[768]{0:T(1024)(128)(2,1)} %get-tuple-element.20) | copy-start | bytes 4612
  193.0 3.6 %copy-start.48 = (bf16[768]{0:T(1024)(128)(2,1)S(1)}, bf16[768]{0:T(1024)(128)(2,1)}, u32[]{:S(2)}) copy-start(bf16[768]{0:T(1024)(128)(2,1)} %get-tuple-element.16) | copy-start | bytes 4612
  193.1 3.7 %copy-start.47 = (bf16[768]{0:T(1024)(128)(2,1)S(1)}, bf16[768]{0:T(1024)(128)(2,1)}, u32[]{:S(2)}) copy-start(bf16[768]{0:T(1024)(128)(2,1)} %get-tuple-element.19) | copy-start | bytes 4612
  (25 other events, 37.4 us)

commit v2 on v1

--- a/solution.py
+++ b/solution.py
@@ -348,16 +348,6 @@
     return matrices, vectors
 
 
-def layer_norm(values, gain, shift):
-    centre = values - jnp.mean(values, axis=-1, keepdims=True)
-    spread = jnp.mean(centre * centre, axis=-1, keepdims=True)
-    return centre * lax.rsqrt(spread + EPSILON) * gain + shift
-
-
-def smooth_gate(values):
-    return jax.nn.gelu(values, approximate=False)
-
-
 def seq_masks(lengths, row_count):
     blocks = lengths.shape[0]
     block_width = row_count // blocks
@@ -380,19 +370,214 @@
     )
 
 
-def column_term(left, right):
-    return outer_sum(left, right)
-
-
 def back_product(grad, weight):
     return lax.dot_general(
         grad, weight, (((1,), (1,)), ((), ())), preferred_element_type=jnp.float32
     )
 
 
-def masked_scores(queries, keys_all, same_seq, factor):
-    raw = jnp.einsum("qhd,khd->hqk", queries, keys_all, preferred_element_type=jnp.float32) * factor
-    return jnp.where(same_seq[None], raw, -1e30)
+def matmul(left, right):
+    return jnp.dot(left, right, preferred_element_type=jnp.float32)
+
+
+def column_sum(values):
+    return jnp.sum(values, axis=0, keepdims=True)
+
+
+def row_mean(values):
+    return jnp.mean(values, axis=-1, keepdims=True)
+
+
+def normalise(values):
+    centre = values - row_mean(values)
+    scale = lax.rsqrt(row_mean(centre * centre) + EPSILON)
+    return centre * scale, scale
+
+
+def norm_back(grad, gain, unit, scale):
+    scaled = grad * gain
+    return scale * (scaled - row_mean(scaled) - unit * row_mean(scaled * unit))
+
+
+def layer_kernel(
+    hidden_ref,
+    cotangent_ref,
+    alive_ref,
+    same_ref,
+    w_qkv,
+    w_out,
+    w_in,
+    w_back,
+    bias_qkv,
+    b_out,
+    gain_one,
+    shift_one,
+    b_in,
+    b_back,
+    gain_two,
+    shift_two,
+    output_ref,
+    grad_hidden_ref,
+    dw_qkv,
+    dw_out,
+    dw_in,
+    dw_back,
+    db_qkv,
+    db_out,
+    dgain_one,
+    dshift_one,
+    db_in,
+    db_back,
+    dgain_two,
+    dshift_two,
+    qkv_ref,
+    probs_ref,
+    attended_ref,
+    unit_one_ref,
+    gated_ref,
+    slope_ref,
+    grad_sum_ref,
+    grad_attended_ref,
+    grad_qkv_ref,
+):
+    low, wide = jnp.bfloat16, jnp.float32
+    rows, width = hidden_ref.shape
+    factor = HEAD_DIM ** (-0.5)
+    pair_width = 2 * HEAD_DIM
+    alive = alive_ref[...]
+    hidden_width = w_in.shape[1]
+    spans = [slice(start, start + width) for start in range(0, hidden_width, width)]
+    left_half = lax.broadcasted_iota(jnp.int32, (rows, pair_width), 1) < HEAD_DIM
+
+    for part in range(3):
+        span = slice(part * width, (part + 1) * width)
+        projected = matmul(hidden_ref[...], w_qkv[:, span]) + bias_qkv[:, span]
+        if part == 0:
+            projected = projected * factor
+        qkv_ref[:, span] = projected.astype(low)
+
+    def pair_span(part, pair):
+        start = part * width + pair * pair_width
+        return slice(start, start + pair_width)
+
+    def halves(values):
+        zero = jnp.zeros_like(values)
+        return jnp.where(left_half, values, zero), jnp.where(left_half, zero, values)
+
+    pairs = width // pair_width
+    for pair in range(pairs):
+        queries = qkv_ref[:, pair_span(0, pair)]
+        keys = qkv_ref[:, pair_span(1, pair)]
+        values = qkv_ref[:, pair_span(2, pair)]
+        found = []
+        for half, part in enumerate(halves(queries)):
+            scores = jnp.where(same_ref[...] > 0, back_product(part, keys), -1e30)
+            expo = jnp.exp(scores - jnp.max(scores, axis=-1, keepdims=True))
+            probs = expo * (1.0 / jnp.sum(expo, axis=-1, keepdims=True))
+            probs_ref[2 * pair + half] = probs
+            found.append(matmul(probs.astype(low), values))
+        attended = jnp.where(left_half, found[0], found[1]) * alive
+        attended_ref[:, pair_span(0, pair)] = attended.astype(low)
+
+    summed_one = hidden_ref[...].astype(wide) + matmul(attended_ref[...], w_out[...]) + b_out[...]
+    unit_one, scale_one = normalise(summed_one)
+    unit_one_ref[...] = unit_one
+    normed_one = unit_one * gain_one[...] + shift_one[...]
+    normed_low = normed_one.astype(low)
+    summed_two = normed_one + b_back[...]
+    for span in spans:
+        inner = matmul(normed_low, w_in[:, span]) + b_in[:, span]
+        below = 0.5 + 0.5 * lax.erf(inner * 0.7071067811865476)
+        slope_ref[:, span] = below + inner * (0.3989422804014327 * jnp.exp(-0.5 * inner * inner))
+        gated = (inner * below).astype(low)
+        gated_ref[:, span] = gated
+        summed_two = summed_two + matmul(gated, w_back[span, :])
+    unit_two, scale_two = normalise(summed_two)
+    output_ref[...] = ((unit_two * gain_two[...] + shift_two[...]) * alive).astype(low)
+
+    grad_out = cotangent_ref[...].astype(wide) * alive
+    dgain_two[...] = column_sum(grad_out * unit_two)
+    dshift_two[...] = column_sum(grad_out)
+    grad_sum_two = norm_back(grad_out, gain_two[...], unit_two, scale_two)
+    branch_two = grad_sum_two.astype(low)
+    db_back[...] = column_sum(branch_two.astype(wide))
+    grad_normed = grad_sum_two
+    for span in spans:
+        dw_back[span, :] = outer_sum(gated_ref[:, span], branch_two).astype(low)
+        grad_inner = (back_product(branch_two, w_back[span, :]) * slope_ref[:, span]).astype(low)
+        db_in[:, span] = column_sum(grad_inner.astype(wide))
+        dw_in[:, span] = outer_sum(normed_low, grad_inner).astype(low)
+        grad_normed = grad_normed + back_product(grad_inner, w_in[:, span])
+    unit_one = unit_one_ref[...]
+    dgain_one[...] = column_sum(grad_normed * unit_one)
+    dshift_one[...] = column_sum(grad_normed)
+    grad_sum_one = norm_back(grad_normed, gain_one[...], unit_one, scale_one)
+    grad_sum_ref[...] = grad_sum_one
+    branch_one = grad_sum_one.astype(low)
+    db_out[...] = column_sum(branch_one.astype(wide))
+    dw_out[...] = outer_sum(attended_ref[...], branch_one).astype(low)
+    grad_attended_ref[...] = (back_product(branch_one, w_out[...]) * alive).astype(low)
+
+    for pair in range(pairs):
+        queries = qkv_ref[:, pair_span(0, pair)]
+        keys = qkv_ref[:, pair_span(1, pair)]
+        values = qkv_ref[:, pair_span(2, pair)]
+        grad_attended = grad_attended_ref[:, pair_span(0, pair)]
+        found = []
+        for half, part in enumerate(halves(grad_attended)):
+            probs = probs_ref[2 * pair + half]
+            grad_probs = back_product(part, values)
+            inner_dot = jnp.sum(probs * grad_probs, axis=-1, keepdims=True)
+            grad_scores = (probs * (grad_probs - inner_dot)).astype(low)
+            found.append(
+                (
+                    matmul(grad_scores, keys) * factor,
+                    outer_sum(grad_scores, queries),
+                    outer_sum(probs.astype(low), grad_attended),
+                )
+            )
+        for part in range(3):
+            joined = jnp.where(left_half, found[0][part], found[1][part])
+            grad_qkv_ref[:, pair_span(part, pair)] = joined.astype(low)
+
+    grad_hidden = grad_sum_ref[...]
+    for part in range(3):
+        span = slice(part * width, (part + 1) * width)
+        grad_part = grad_qkv_ref[:, span]
+        db_qkv[:, span] = column_sum(grad_part.astype(wide))
+        dw_qkv[:, span] = outer_sum(hidden_ref[...], grad_part).astype(low)
+        grad_hidden = grad_hidden + back_product(grad_part, w_qkv[:, span])
+    grad_hidden_ref[...] = grad_hidden.astype(low)
+
+
+def layer(hidden, cotangent, alive, same, weights, lines):
+    rows, width = hidden.shape
+    heads, hidden_width = width // HEAD_DIM, weights[2].shape[1]
+    low, wide = jnp.bfloat16, jnp.float32
+    shape = jax.ShapeDtypeStruct
+    outs = (
+        [shape(hidden.shape, low)] * 2
+        + [shape(weight.shape, low) for weight in weights]
+        + [shape(line.shape, wide) for line in lines]
+    )
+    return pl.pallas_call(
+        layer_kernel,
+        out_shape=outs,
+        in_specs=[pl.BlockSpec(memory_space=pltpu.VMEM)] * (4 + len(weights) + len(lines)),
+        out_specs=[pl.BlockSpec(memory_space=pltpu.VMEM)] * len(outs),
+        scratch_shapes=[
+            pltpu.VMEM((rows, 3 * width), low),
+            pltpu.VMEM((heads, rows, rows), wide),
+            pltpu.VMEM((rows, width), low),
+            pltpu.VMEM((rows, width), wide),
+            pltpu.VMEM((rows, hidden_width), low),
+            pltpu.VMEM((rows, hidden_width), wide),
+            pltpu.VMEM((rows, width), wide),
+            pltpu.VMEM((rows, width), low),
+            pltpu.VMEM((rows, 3 * width), low),
+        ],
+        compiler_params=pltpu.CompilerParams(vmem_limit_bytes=VMEM_LIMIT),
+    )(hidden, cotangent, alive, same, *weights, *lines)
 
 
 def shards(
@@ -413,8 +598,6 @@
     shift_two,
 ):
     row_count, model_width = hidden.shape
-    head_count = model_width // HEAD_DIM
-    factor = HEAD_DIM ** (-0.5)
     alive_row, same_seq = seq_masks(seq_lengths, row_count)
     alive_col = alive_row.astype(jnp.float32)[:, None]
     count = lax.axis_size("fsdp")
@@ -441,126 +624,42 @@
         full_gtwo,
         full_stwo,
     ) = full_biases
-    bias_qv = full_bqv.astype(jnp.float32)
     bias_qkv = jnp.concatenate(
-        [bias_qv[:model_width], jnp.zeros((model_width,), jnp.float32), bias_qv[model_width:]]
-    )
-    qkv_low = (jnp.dot(hidden, full_qkv, preferred_element_type=jnp.float32) + bias_qkv).astype(
-        jnp.bfloat16
-    )
-    queries = qkv_low[:, :model_width].reshape(row_count, head_count, HEAD_DIM)
-    keys_all = qkv_low[:, model_width : 2 * model_width].reshape(row_count, head_count, HEAD_DIM)
-    values_all = qkv_low[:, 2 * model_width :].reshape(row_count, head_count, HEAD_DIM)
-    scores = masked_scores(queries, keys_all, same_seq, factor)
-    highest = jnp.max(scores, axis=-1, keepdims=True)
-    expo = jnp.exp(scores - highest)
-    totals = jnp.sum(expo, axis=-1, keepdims=True)
-    log_total = highest + jnp.log(totals)
-    probs_low = (expo / totals).astype(jnp.bfloat16)
-    attended = jnp.einsum(
-        "hqk,khd->qhd", probs_low, values_all, preferred_element_type=jnp.float32
-    ).reshape(row_count, model_width)
-    attended_low = (attended * alive_col).astype(jnp.bfloat16)
-    summed_one = (
-        hidden.astype(jnp.float32)
-        + jnp.dot(attended_low, full_out, preferred_element_type=jnp.float32)
-        + full_bout.astype(jnp.float32)
-    )
-    normed_one = layer_norm(
-        summed_one, full_gone.astype(jnp.float32), full_sone.astype(jnp.float32)
-    )
-    normed_low = normed_one.astype(jnp.bfloat16)
-    inner = jnp.dot(normed_low, full_in, preferred_element_type=jnp.float32) + full_bin.astype(
-        jnp.float32
-    )
-    gated_low = smooth_gate(inner).astype(jnp.bfloat16)
-    summed_two = (
-        normed_one
-        + jnp.dot(gated_low, full_back, preferred_element_type=jnp.float32)
-        + full_bback.astype(jnp.float32)
-    )
-    output = (
-        layer_norm(summed_two, full_gtwo.astype(jnp.float32), full_stwo.astype(jnp.float32))
-        * alive_col
-    ).astype(jnp.bfloat16)
-    shift_zero = jnp.zeros((model_width,), jnp.float32)
-    unused, norm_two_back = jax.vjp(
-        layer_norm, summed_two, full_gtwo.astype(jnp.float32), shift_zero
-    )
-    grad_sum_two, grad_gtwo, grad_stwo = norm_two_back(cotangent.astype(jnp.float32) * alive_col)
-    grad_branch_two = grad_sum_two.astype(jnp.bfloat16)
-    term_bback = jnp.sum(grad_branch_two.astype(jnp.float32), axis=0)
-    grad_gated = back_product(grad_branch_two, full_back)
-    unused, gate_back = jax.vjp(smooth_gate, inner)
-    grad_inner = gate_back(grad_gated)[0].astype(jnp.bfloat16)
-    term_bin = jnp.sum(grad_inner.astype(jnp.float32), axis=0)
-    grad_normed = grad_sum_two + back_product(grad_inner, full_in)
-    unused, norm_one_back = jax.vjp(
-        layer_norm, summed_one, full_gone.astype(jnp.float32), shift_zero
-    )
-    grad_sum_one, grad_gone, grad_sone = norm_one_back(grad_normed)
-    grad_branch_one = grad_sum_one.astype(jnp.bfloat16)
-    term_bout = jnp.sum(grad_branch_one.astype(jnp.float32), axis=0)
-    grad_attended = (
-        (back_product(grad_branch_one, full_out) * alive_col)
-        .astype(jnp.bfloat16)
-        .reshape(row_count, head_count, HEAD_DIM)
-    )
-    scores_again = masked_scores(queries, keys_all, same_seq, factor)
-    probs = jnp.exp(scores_again - log_total)
-    probs_again_low = probs.astype(jnp.bfloat16)
-    grad_probs = jnp.einsum(
-        "qhd,khd->hqk", grad_attended, values_all, preferred_element_type=jnp.float32
-    )
-    inner_dot = jnp.sum(probs * grad_probs, axis=-1, keepdims=True)
-    grad_scores = jnp.where(same_seq[None], probs * (grad_probs - inner_dot), 0.0).astype(
-        jnp.bfloat16
-    )
-    grad_queries = (
-        jnp.einsum("hqk,khd->qhd", grad_scores, keys_all, preferred_element_type=jnp.float32)
-        * factor
-    )
-    grad_keys = (
-        jnp.einsum("hqk,qhd->khd", grad_scores, queries, preferred_element_type=jnp.float32)
-        * factor
-    )
-    grad_values = jnp.einsum(
-        "hqk,qhd->khd", probs_again_low, grad_attended, preferred_element_type=jnp.float32
-    )
-    grad_qkv = jnp.concatenate(
         [
-            grad_queries.reshape(row_count, model_width),
-            grad_keys.reshape(row_count, model_width),
-            grad_values.reshape(row_count, model_width),
-        ],
-        axis=1,
-    ).astype(jnp.bfloat16)
-    column_sums = jnp.sum(grad_qkv.astype(jnp.float32), axis=0)
-    term_bqv = jnp.concatenate([column_sums[:model_width], column_sums[2 * model_width :]])
-    grad_hidden = (grad_sum_one + back_product(grad_qkv, full_qkv)).astype(jnp.bfloat16)
+            full_bqv[:model_width],
+            jnp.zeros((model_width,), full_bqv.dtype),
+            full_bqv[model_width:],
+        ]
+    )
+    lines = [
+        line.astype(jnp.float32)[None]
+        for line in (
+            bias_qkv,
+            full_bout,
+            full_gone,
+            full_sone,
+            full_bin,
+            full_bback,
+            full_gtwo,
+            full_stwo,
+        )
+    ]
+    results = layer(
+        hidden,
+        cotangent,
+        alive_col,
+        same_seq.astype(jnp.float32),
+        (full_qkv, full_out, full_in, full_back),
+        lines,
+    )
+    output, grad_hidden = results[:2]
+    weight_terms, line_terms = results[2:6], [line[0] for line in results[6:]]
+    line_terms[0] = jnp.concatenate(
+        [line_terms[0][:model_width], line_terms[0][2 * model_width :]]
+    )
     terms = pack(
-        [
-            column_term(left, right).reshape(count, -1, right.shape[1])
-            for left, right in (
-                (hidden, grad_qkv),
-                (attended_low, grad_branch_one),
-                (normed_low, grad_inner),
-                (gated_low, grad_branch_two),
-            )
-        ],
-        [
-            vector.reshape(count, -1)
-            for vector in (
-                term_bqv,
-                term_bout,
-                grad_gone,
-                grad_sone,
-                term_bin,
-                term_bback,
-                grad_gtwo,
-                grad_stwo,
-            )
-        ],
+        [term.reshape(count, -1, term.shape[1]) for term in weight_terms],
+        [line.reshape(count, -1) for line in line_terms],
         model_width,
         jnp.bfloat16,
     )

time: 312 us -> 270 us (0.87)
  matrix products: 56.8 us -> 0 us
  Pallas kernels: 184 us -> 210 us
  other arithmetic: 16.5 us -> 10.2 us
  local copies, waits for them, and re-layouts: 52.1 us -> 47.8 us
    dot_general x18 -> x0, matrix products: 56.8 us -> none  [the longest x4 14.5 us: back_product(): lax.dot_general(grad, weight, (((1,), (1,)), ((), ())), preferred_element...]
    pallas_call x0 -> x1, Pallas kernels: none -> 26.6 us  [layer(): pl.pallas_call(layer_kernel, out_shape=outs, in_specs=[pl.BlockSpec(memor...]
    reduce_sum x9 -> x0, other arithmetic: 9.83 us -> none  [the longest x1 3.08 us: layer_norm(): return centre * lax.rsqrt(spread + EPSILON) * gain + shift]
    concatenate x2 -> x4, other arithmetic: 1.43 us -> 6.06 us  [unpack(): matrices.append(jnp.concatenate(chunks, axis=1))]
    unnamed x135 -> x56, local copies, waits for them, and re-layouts: 23 us -> 26.4 us
    convert_element_type x8 -> x7, local copies, waits for them, and re-layouts: 7.08 us -> 4.77 us  [shards(): line.astype(jnp.float32)[None]]
where the time goes in v2:
time: 270 us; the launch traced here: 269 us
  Pallas kernels  210 us (78%)
  local copies, waits for them, and re-layouts  47.8 us (18%)
  other arithmetic  10.2 us (4%)
    pallas_call x1, Pallas kernels, scatter_blocks(): pl.pallas_call(functools.partial(scatter_kernel, side, depth), out_shape=...  105 us
    pallas_call x1, Pallas kernels, gather_blocks(): pl.pallas_call(functools.partial(gather_kernel, side, depth), out_shape=j...  78.9 us
    pallas_call x1, Pallas kernels, layer(): pl.pallas_call(layer_kernel, out_shape=outs, in_specs=[pl.BlockSpec(memor...  26.6 us
    unnamed x56, local copies, waits for them, and re-layouts  26.4 us
    slice x2, local copies, waits for them, and re-layouts, unpack(): chunks.append(blocks[:, row:row + rows, :].reshape(count * rows, width))  8.03 us
    concatenate x4, other arithmetic, unpack(): matrices.append(jnp.concatenate(chunks, axis=1))  6.06 us

profile of v2, /device:TPU:3, one launch (start us, length us, event | category | flops | bytes accessed | tf_op | source)
XLA Modules:
  0.0 269.3 jit_solution(15651842350118652477)
XLA Ops:
  3.3 0.8 and_convert_fusion.same_ref
  4.1 0.8 constant_dynamic-update-slice_fusion.8
  4.9 0.8 constant_dynamic-update-slice_fusion.7
  5.7 0.8 constant_dynamic-update-slice_fusion.6
  6.4 0.8 constant_dynamic-update-slice_fusion.5
  7.2 0.8 constant_dynamic-update-slice_fusion.4
  8.0 0.8 constant_dynamic-update-slice_fusion.3
  8.7 0.8 constant_dynamic-update-slice_fusion.2
  10.3 0.9 bitcast_dynamic-update-slice_fusion
  11.2 0.9 concatenate.47
  13.0 78.9 %shard_map.254 = bf16[32,304,768]{2,1,0:T(8,128)(2,1)} custom-call(bf16[304,768]{1,0:T(8,128)(2,1)} %bitcast.106), custom_call_target="tpu_custom_call" | custom-call | tf_op jit(solution)/shard_map/pallas_call | solution.py:154
  91.9 5.2 %fusion.5 = (bf16[32,24,768]{2,1,0:T(8,128)(2,1)S(1)}, bf16[32,24,768]{2,1,0:T(8,128)(2,1)S(1)}, bf16[32,24,768]{2,1,0:T(8,128)(2,1)S(1)}, bf16[32,24,768]{2,1,0...) fusion(bf16[32,304,768]{2,1,0:T(8,128)(2,1)} %shard_map.254), kind=kLoop, calls=%fused_computation.78 | loop fusion | bytes 18874368 | tf_op jit(solution)/shard_map/slice | solution.py:340
  97.1 1.9 pad_maximum_fusion.1.w_qkv
  99.1 2.7 %pad_maximum_fusion.w_in = bf16[768,3072]{1,0:T(8,128)(2,1)} fusion(bf16[768,768]{1,0:T(8,128)(2,1)S(1)} %bitcast.81, bf16[768,768]{1,0:T(8,128)(2,1)S(1)} %bitcast.82, bf16[768,768]{1,0:T(8,128)(2,1)S(1)} %bitcast.83, bf16[768,768]{1,0:T(8,128)(2,1)S(1)} %bitcast.80), kind=kLoop, calls=%fused_computation | loop fusion | flops 18874368 | bytes 9437184 | tf_op jit(solution)/shard_map/concatenate | solution.py:342
  101.8 0.8 slice-done.2
  102.6 0.9 slice-done.3
  103.5 2.8 %slice.183 = bf16[32,96,768]{2,1,0:T(8,128)(2,1)} slice(bf16[32,304,768]{2,1,0:T(8,128)(2,1)S(1)} %bitcast.76), slice={[0:32], [192:288], [0:768]} | slice | bytes 9437184 | tf_op jit(solution)/shard_map/slice | solution.py:340
  112.3 26.6 %shard_map.255 = (bf16[256,768]{1,0:T(8,128)(2,1)}, bf16[256,768]{1,0:T(8,128)(2,1)}, bf16[768,2304]{1,0:T(8,128)(2,1)}, bf16[768,768]{1,0:T(8,128)(2,1)}, bf16[...) custom-call(bf16[256,768]{1,0:T(8,128)(2,1)} %hidden_ref.1, ...), custom_call_target="tpu_custom_call" | custom-call | tf_op jit(solution)/shard_map/pallas_call | solution.py:563
  138.9 2.5 slice_dynamic-update-slice_fusion.6
  141.4 2.4 slice_dynamic-update-slice_fusion.5
  143.8 2.5 slice_dynamic-update-slice_fusion.4
  146.3 1.1 constant_dynamic-update-slice_fusion.11
  147.4 1.2 slice_dynamic-update-slice_fusion.3
  148.6 1.2 slice_dynamic-update-slice_fusion.2
  149.7 1.1 slice_dynamic-update-slice_fusion.1
  150.9 1.2 slice_dynamic-update-slice_fusion
  152.1 2.4 constant_dynamic-update-slice_fusion.10
  155.9 1.0 constant_dynamic-update-slice_fusion.9.terms
  156.9 104.9 %shard_map.256 = f32[304,768]{1,0:T(8,128)} custom-call(bf16[32,304,768]{2,1,0:T(8,128)(2,1)} %constant_dynamic-update-slice_fusion.9.terms), custom_call_target="tpu_custom_call" | custom-call | tf_op jit(solution)/shard_map/pallas_call | solution.py:293
  261.8 1.8 slice_bitcast_fusion.4
  264.3 0.8 slice_bitcast_fusion.9
  267.6 1.7 slice_bitcast_fusion
  (92 shorter events, 14.8 us)
Async XLA Ops:
  12.2 0.8 copy-start.2
  91.9 9.9 %slice-start = ((s8[14942208]{0:T(1024)(128)(4,1)}), s8[4194304]{0:T(1024)(128)(4,1)S(1)}, s32[]{:S(2)}) async-start(s8[14942208]{0:T(1024)(128)(4,1)} %bitcast.75), calls=%async_computation | async-start | bytes 8388608
  91.9 9.9 %slice-start.1 = ((s8[14942208]{0:T(1024)(128)(4,1)}), s8[4194304]{0:T(1024)(128)(4,1)S(1)}, s32[]{:S(2)}) async-start(s8[14942208]{0:T(1024)(128)(4,1)} %bitcast.75), calls=%async_computation.1 | async-start | bytes 8388608
  91.9 10.7 %slice-start.2 = ((s8[14942208]{0:T(1024)(128)(4,1)}), s8[4194304]{0:T(1024)(128)(4,1)S(1)}, s32[]{:S(2)}) async-start(s8[14942208]{0:T(1024)(128)(4,1)} %bitcast.75), calls=%async_computation.2 | async-start | bytes 8388608
  99.1 4.4 %slice-start.3 = ((s8[14942208]{0:T(1024)(128)(4,1)}), s8[2359296]{0:T(1024)(128)(4,1)S(1)}, s32[]{:S(2)}) async-start(s8[14942208]{0:T(1024)(128)(4,1)} %bitcast.75), calls=%async_computation.3 | async-start | bytes 4718592
  103.5 2.8 %slice-start.4 = ((bf16[32,304,768]{2,1,0:T(8,128)(2,1)}), bf16[32,16,768]{2,1,0:T(8,128)(2,1)S(1)}, s32[]{:S(2)}) async-start(bf16[32,304,768]{2,1,0:T(8,128)(2,1)} %shard_map.254), calls=%async_computation.4 | async-start | bytes 1572864 | tf_op jit(solution)/shard_map/slice | solution.py:343
  138.8 7.4 %copy-start.1 = (bf16[768,768]{1,0:T(8,128)(2,1)S(1)}, bf16[768,768]{1,0:T(8,128)(2,1)}, u32[]{:S(2)}) copy-start(bf16[768,768]{1,0:T(8,128)(2,1)} %get-tuple-element.31) | copy-start | bytes 3538948
  138.9 8.5 %copy-start = (bf16[768,3072]{1,0:T(8,128)(2,1)S(1)}, bf16[768,3072]{1,0:T(8,128)(2,1)}, u32[]{:S(2)}) copy-start(bf16[768,3072]{1,0:T(8,128)(2,1)} %get-tuple-element.32) | copy-start | bytes 14155780
  143.8 8.3 %slice-start.5 = ((s8[4718592]{0:T(1024)(128)(4,1)}), s8[4194304]{0:T(1024)(128)(4,1)S(1)}, s32[]{:S(2)}) async-start(s8[4718592]{0:T(1024)(128)(4,1)} %bitcast.87), calls=%async_computation.5 | async-start | bytes 8388608
  147.4 4.6 %slice-start.6 = ((s8[4718592]{0:T(1024)(128)(4,1)}), s8[524288]{0:T(1024)(128)(4,1)S(1)}, s32[]{:S(2)}) async-start(s8[4718592]{0:T(1024)(128)(4,1)} %bitcast.87), calls=%async_computation.6 | async-start | bytes 1048576
  152.0 2.5 copy-start.4
  152.0 2.7 %copy-start.9 = (f32[1,768]{1,0:T(1,128)S(1)}, f32[1,768]{1,0:T(1,128)}, u32[]{:S(2)}) copy-start(f32[1,768]{1,0:T(1,128)} %get-tuple-element.35) | copy-start | bytes 9220
  152.0 2.7 %copy-start.10 = (f32[1,768]{1,0:T(1,128)S(1)}, f32[1,768]{1,0:T(1,128)}, u32[]{:S(2)}) copy-start(f32[1,768]{1,0:T(1,128)} %get-tuple-element.36) | copy-start | bytes 9220
  152.0 2.9 %copy-start.7 = (f32[1,768]{1,0:T(1,128)S(1)}, f32[1,768]{1,0:T(1,128)}, u32[]{:S(2)}) copy-start(f32[1,768]{1,0:T(1,128)} %get-tuple-element.37) | copy-start | bytes 9220
  152.1 2.9 %copy-start.8 = (f32[1,768]{1,0:T(1,128)S(1)}, f32[1,768]{1,0:T(1,128)}, u32[]{:S(2)}) copy-start(f32[1,768]{1,0:T(1,128)} %get-tuple-element.39) | copy-start | bytes 9220
  152.1 3.1 %copy-start.3 = (f32[1,3072]{1,0:T(1,128)S(1)}, f32[1,3072]{1,0:T(1,128)}, u32[]{:S(2)}) copy-start(f32[1,3072]{1,0:T(1,128)} %get-tuple-element.38) | copy-start | bytes 36868
  152.1 3.3 %copy-start.5 = (f32[1,768]{1,0:T(1,128)S(1)}, f32[1,768]{1,0:T(1,128)}, u32[]{:S(2)}) copy-start(f32[1,768]{1,0:T(1,128)} %get-tuple-element.40) | copy-start | bytes 9220
  152.1 3.3 %copy-start.6 = (f32[1,768]{1,0:T(1,128)S(1)}, f32[1,768]{1,0:T(1,128)}, u32[]{:S(2)}) copy-start(f32[1,768]{1,0:T(1,128)} %get-tuple-element.41) | copy-start | bytes 9220

commit v3 on v2

--- a/solution.py
+++ b/solution.py
@@ -397,6 +397,65 @@
 def norm_back(grad, gain, unit, scale):
     scaled = grad * gain
     return scale * (scaled - row_mean(scaled) - unit * row_mean(scaled * unit))
+
+
+class Chunks:
+    def __init__(self, blocks, row, shape):
+        self.blocks, self.row = blocks, row
+        self.rows, self.columns = shape
+        self.width = blocks.shape[2]
+
+    def where(self, key):
+        if key is Ellipsis:
+            key = (slice(None), slice(0, self.width))
+        height, span = key
+        if self.columns > self.width:
+            start = self.row + span.start // self.width * self.rows
+            return slice(None), slice(start, start + self.rows)
+        devices = slice(None)
+        if height.start is not None:
+            devices = slice(height.start // self.rows, height.stop // self.rows)
+        return devices, slice(self.row, self.row + self.rows)
+
+    def __setitem__(self, key, value):
+        devices, rows = self.where(key)
+        parts = value.reshape(-1, self.rows, self.width)
+        self.blocks[devices, rows, :] = parts.astype(self.blocks.dtype)
+
+    def __getitem__(self, key):
+        devices, rows = self.where(key)
+        parts = self.blocks[devices, rows, :]
+        if self.rows % 16 != 0:
+            parts = parts.astype(jnp.float32)
+        return parts.reshape(-1, self.width).astype(self.blocks.dtype)
+
+
+class Cast:
+    def __init__(self, ref):
+        self.ref = ref
+
+    def __setitem__(self, key, value):
+        self.ref[key] = value.astype(self.ref.dtype)
+
+
+def dense_kernel(*refs):
+    layer_kernel(*refs[:18], *[Cast(ref) for ref in refs[18:22]], *refs[22:])
+
+
+def packed_kernel(shapes, *refs):
+    blocks, terms = refs[4], refs[15]
+    weights, grads, row = [], [], 0
+    for shape in shapes:
+        weights.append(Chunks(blocks, row, shape))
+        grads.append(Chunks(terms, row, shape))
+        row += shape[0] * (shape[1] // blocks.shape[2])
+    width = blocks.shape[2]
+    for index, dense in enumerate(refs[33:36]):
+        for start in range(0, dense.shape[1], width):
+            span = slice(start, start + width)
+            dense[:, span] = weights[index][:, span]
+        weights[index] = dense
+    layer_kernel(*refs[:4], *weights, *refs[5:15], *grads, *refs[16:33])
 
 
 def layer_kernel(
@@ -445,7 +504,7 @@
     factor = HEAD_DIM ** (-0.5)
     pair_width = 2 * HEAD_DIM
     alive = alive_ref[...]
-    hidden_width = w_in.shape[1]
+    hidden_width = gated_ref.shape[1]
     spans = [slice(start, start + width) for start in range(0, hidden_width, width)]
     left_half = lax.broadcasted_iota(jnp.int32, (rows, pair_width), 1) < HEAD_DIM
 
@@ -503,10 +562,10 @@
     db_back[...] = column_sum(branch_two.astype(wide))
     grad_normed = grad_sum_two
     for span in spans:
-        dw_back[span, :] = outer_sum(gated_ref[:, span], branch_two).astype(low)
+        dw_back[span, :] = outer_sum(gated_ref[:, span], branch_two)
         grad_inner = (back_product(branch_two, w_back[span, :]) * slope_ref[:, span]).astype(low)
         db_in[:, span] = column_sum(grad_inner.astype(wide))
-        dw_in[:, span] = outer_sum(normed_low, grad_inner).astype(low)
+        dw_in[:, span] = outer_sum(normed_low, grad_inner)
         grad_normed = grad_normed + back_product(grad_inner, w_in[:, span])
     unit_one = unit_one_ref[...]
     dgain_one[...] = column_sum(grad_normed * unit_one)
@@ -515,7 +574,7 @@
     grad_sum_ref[...] = grad_sum_one
     branch_one = grad_sum_one.astype(low)
     db_out[...] = column_sum(branch_one.astype(wide))
-    dw_out[...] = outer_sum(attended_ref[...], branch_one).astype(low)
+    dw_out[...] = outer_sum(attended_ref[...], branch_one)
     grad_attended_ref[...] = (back_product(branch_one, w_out[...]) * alive).astype(low)
 
     for pair in range(pairs):
@@ -545,14 +604,14 @@
         span = slice(part * width, (part + 1) * width)
         grad_part = grad_qkv_ref[:, span]
         db_qkv[:, span] = column_sum(grad_part.astype(wide))
-        dw_qkv[:, span] = outer_sum(hidden_ref[...], grad_part).astype(low)
+        dw_qkv[:, span] = outer_sum(hidden_ref[...], grad_part)
         grad_hidden = grad_hidden + back_product(grad_part, w_qkv[:, span])
     grad_hidden_ref[...] = grad_hidden.astype(low)
 
 
-def layer(hidden, cotangent, alive, same, weights, lines):
+def layer(hidden, cotangent, alive, same, weights, lines, shapes=None):
     rows, width = hidden.shape
-    heads, hidden_width = width // HEAD_DIM, weights[2].shape[1]
+    heads, hidden_width = width // HEAD_DIM, lines[4].shape[1]
     low, wide = jnp.bfloat16, jnp.float32
     shape = jax.ShapeDtypeStruct
     outs = (
@@ -560,22 +619,28 @@
         + [shape(weight.shape, low) for weight in weights]
         + [shape(line.shape, wide) for line in lines]
     )
+    scratch = [
+        pltpu.VMEM((rows, 3 * width), low),
+        pltpu.VMEM((heads, rows, rows), wide),
+        pltpu.VMEM((rows, width), low),
+        pltpu.VMEM((rows, width), wide),
+        pltpu.VMEM((rows, hidden_width), low),
+        pltpu.VMEM((rows, hidden_width), wide),
+        pltpu.VMEM((rows, width), wide),
+        pltpu.VMEM((rows, width), low),
+        pltpu.VMEM((rows, 3 * width), low),
+    ]
+    kernel = dense_kernel
+    if shapes is not None:
+        kernel = functools.partial(packed_kernel, shapes)
+        count = weights[0].shape[0]
+        scratch += [pltpu.VMEM((count * part[0], part[1]), low) for part in shapes[:3]]
     return pl.pallas_call(
-        layer_kernel,
+        kernel,
         out_shape=outs,
         in_specs=[pl.BlockSpec(memory_space=pltpu.VMEM)] * (4 + len(weights) + len(lines)),
         out_specs=[pl.BlockSpec(memory_space=pltpu.VMEM)] * len(outs),
-        scratch_shapes=[
-            pltpu.VMEM((rows, 3 * width), low),
-            pltpu.VMEM((heads, rows, rows), wide),
-            pltpu.VMEM((rows, width), low),
-            pltpu.VMEM((rows, width), wide),
-            pltpu.VMEM((rows, hidden_width), low),
-            pltpu.VMEM((rows, hidden_width), wide),
-            pltpu.VMEM((rows, width), wide),
-            pltpu.VMEM((rows, width), low),
-            pltpu.VMEM((rows, 3 * width), low),
-        ],
+        scratch_shapes=scratch,
         compiler_params=pltpu.CompilerParams(vmem_limit_bytes=VMEM_LIMIT),
     )(hidden, cotangent, alive, same, *weights, *lines)
 
@@ -611,8 +676,13 @@
         model_width,
         jnp.bfloat16,
     )[0]
-    (full_qkv, full_out, full_in, full_back), full_biases = unpack(
-        gather_blocks(block, count), weight_shapes, bias_sizes
+    blocks = gather_blocks(block, count)
+    full_weights, full_biases = unpack(blocks, weight_shapes, bias_sizes)
+    used = sum(shape[0] * (shape[1] // model_width) for shape in weight_shapes)
+    in_blocks = (
+        all(shape[0] % 8 == 0 for shape in weight_shapes)
+        and w_back.shape[0] % 16 == 0
+        and used % 16 == 0
     )
     (
         full_bqv,
@@ -644,25 +714,27 @@
             full_stwo,
         )
     ]
-    results = layer(
-        hidden,
-        cotangent,
-        alive_col,
-        same_seq.astype(jnp.float32),
-        (full_qkv, full_out, full_in, full_back),
-        lines,
-    )
+    same = same_seq.astype(jnp.float32)
+    if in_blocks:
+        results = layer(hidden, cotangent, alive_col, same, (blocks,), lines, weight_shapes)
+    else:
+        results = layer(hidden, cotangent, alive_col, same, full_weights, lines)
     output, grad_hidden = results[:2]
-    weight_terms, line_terms = results[2:6], [line[0] for line in results[6:]]
+    line_terms = [line[0] for line in results[-len(lines) :]]
     line_terms[0] = jnp.concatenate(
         [line_terms[0][:model_width], line_terms[0][2 * model_width :]]
     )
-    terms = pack(
-        [term.reshape(count, -1, term.shape[1]) for term in weight_terms],
-        [line.reshape(count, -1) for line in line_terms],
-        model_width,
-        jnp.bfloat16,
-    )
+    line_terms = [line.reshape(count, -1) for line in line_terms]
+    if in_blocks:
+        tail = pack([], line_terms, model_width, jnp.bfloat16)
+        terms = lax.dynamic_update_slice(results[2], tail, (0, used, 0))
+    else:
+        terms = pack(
+            [term.reshape(count, -1, term.shape[1]) for term in results[2:6]],
+            line_terms,
+            model_width,
+            jnp.bfloat16,
+        )
     (share_qkv, share_out, share_in, share_back), vectors = unpack(
         scatter_blocks(terms)[None], weight_shapes, bias_sizes
     )

time: 270 us -> 249 us (0.922)
  local copies, waits for them, and re-layouts: 47.8 us -> 23.6 us
  Pallas kernels: 210 us -> 214 us
    unnamed x56 -> x15, local copies, waits for them, and re-layouts: 26.4 us -> 9.07 us
    slice x2 -> x0, local copies, waits for them, and re-layouts: 8.03 us -> none  [unpack(): chunks.append(blocks[:, row:row + rows, :].reshape(count * rows, width))]
    concatenate x4 -> x2, other arithmetic: 6.06 us -> 1.43 us  [unpack(): matrices.append(jnp.concatenate(chunks, axis=1))]
    pallas_call x1, Pallas kernels: 26.6 us -> 30.3 us  [layer(): pl.pallas_call(kernel, out_shape=outs, in_specs=[pl.BlockSpec(memory_spac...]
    convert_element_type x4, other arithmetic: 0.14 us -> 2.89 us  [pack(): line = jnp.concatenate([vector.astype(dtype) for vector in vectors], axis=1)]
where the time goes in v3:
time: 249 us; the launch traced here: 247 us
  Pallas kernels  214 us (86%)
  local copies, waits for them, and re-layouts  23.6 us (9%)
  other arithmetic  8.97 us (4%)
    pallas_call x1, Pallas kernels, scatter_blocks(): pl.pallas_call(functools.partial(scatter_kernel, side, depth), out_shape=...  105 us
    pallas_call x1, Pallas kernels, gather_blocks(): pl.pallas_call(functools.partial(gather_kernel, side, depth), out_shape=j...  78.9 us
    pallas_call x1, Pallas kernels, layer(): pl.pallas_call(kernel, out_shape=outs, in_specs=[pl.BlockSpec(memory_spac...  30.3 us
    unnamed x15, local copies, waits for them, and re-layouts  9.07 us

profile of v3, /device:TPU:3, one launch (start us, length us, event | category | flops | bytes accessed | tf_op | source)
XLA Modules:
  0.0 247.4 jit_solution(5069139663969588412)
XLA Ops:
  1.6 0.7 fusion.3
  2.3 0.9 concatenate.38
  4.3 0.8 and_convert_fusion.refs_3_
  5.1 0.8 slice_dynamic-update-slice_fusion.6
  5.9 0.8 slice_dynamic-update-slice_fusion.5
  6.6 0.8 slice_dynamic-update-slice_fusion.4
  7.4 0.8 bitcast_dynamic-update-slice_fusion.1
  8.2 0.8 slice_dynamic-update-slice_fusion.3
  9.0 0.8 slice_dynamic-update-slice_fusion.2
  9.7 0.8 slice_dynamic-update-slice_fusion.1
  10.5 0.8 slice_dynamic-update-slice_fusion
  11.3 0.9 bitcast_dynamic-update-slice_fusion
  12.2 0.8 copy-done
  13.0 78.9 %shard_map.254.refs_4_ = bf16[32,304,768]{2,1,0:T(8,128)(2,1)} custom-call(bf16[304,768]{1,0:T(8,128)(2,1)} %bitcast.71), custom_call_target="tpu_custom_call" | custom-call | tf_op jit(solution)/shard_map/pallas_call | solution.py:154
  91.9 1.2 slice.127
  94.3 0.7 reshape.365.refs_9_
  97.0 0.7 reshape.364.refs_8_
  97.7 0.7 reshape.363.refs_7_
  98.4 0.7 reshape.362.refs_6_
  99.1 30.3 %shard_map.255 = (bf16[256,768]{1,0:T(8,128)(2,1)}, bf16[256,768]{1,0:T(8,128)(2,1)}, bf16[32,304,768]{2,1,0:T(8,128)(2,1)}, f32[1,2304]{1,0:T(1,128)}, f32[1,76...) custom-call(bf16[256,768]{1,0:T(8,128)(2,1)} %refs_0_.1, ...), custom_call_target="tpu_custom_call" | custom-call | tf_op jit(solution)/shard_map/pallas_call | solution.py:638
  129.3 0.7 convert_reduce_fusion.5
  130.0 0.7 convert_reduce_fusion.3
  130.7 0.7 convert_reduce_fusion.1
  131.8 0.8 convert_reduce_fusion
  132.9 0.7 convert.15
  134.1 1.0 constant_dynamic-update-slice_fusion.1.terms
  135.1 104.9 %shard_map.256 = f32[304,768]{1,0:T(8,128)} custom-call(bf16[32,304,768]{2,1,0:T(8,128)(2,1)} %constant_dynamic-update-slice_fusion.1.terms), custom_call_target="tpu_custom_call" | custom-call | tf_op jit(solution)/shard_map/pallas_call | solution.py:293
  239.9 0.8 slice_bitcast_fusion.9
  242.5 1.7 slice_bitcast_fusion
  244.2 1.8 slice_bitcast_fusion.4
  246.0 0.7 pad_maximum_fusion
  246.7 0.7 pad_maximum_fusion.1
  (44 shorter events, 8.1 us)
Async XLA Ops:
  12.2 0.8 copy-start
